TPU v7x, 512 devices: a whole 4x8x8 slice. The times are simulated.
512 devices in a mesh: pool: 16 (over x, z_lo, core), tp: 8 (over y), req: 4 (over z_hi).
Axes of the slice: x: 4, y: 8, z: 8 (z_hi: 4, z_lo: 2; z = z_hi * 2 + z_lo), core: 2. Of those that a mesh axis runs over, the one named last changes fastest.
Arguments:
- hidden_in: bfloat16 [4, 2048, 8192], P('req', 'pool', 'tp'), may hold values from -6 to 6
- base_query_rotated: bfloat16 [4, 2048, 8192], P('req', 'pool', 'tp'), may hold values from -6 to 6
- suffix_cache: bfloat16 [4, 2, 2048, 1024], P('req', None, 'pool', 'tp'), may hold values from -6 to 6
- cache_pool: bfloat16 [320, 2, 128, 1024], P('pool', None, None, 'tp'), may hold values from -6 to 6
- adapter_down: bfloat16 [8, 8192, 16], P(None, 'tp'), may hold values from -0.0625 to 0.0625
- adapter_up: bfloat16 [8, 16, 8192], P(None, None, 'tp'), may hold values from -1.5 to 1.5
- block_table: int32 [4, 32], replicated, may hold values from 0 to 319, as said below
- prefix_lengths: int32 [4], replicated, may hold values from 1024 to 4096, as said below
- suffix_lengths: int32 [4], replicated, may hold values from 512 to 2048, as said below
- tenant_adapter: int32 [4], replicated, may hold values from 0 to 7
- write_slots: int32 [4, 16], replicated, may hold values from 0 to 319, as said below
Outputs:
- attended: bfloat16 [4, 2048, 8192], P('req', 'pool', 'tp')
- pool_after: bfloat16 [320, 2, 128, 1024], P('pool', None, None, 'tp')
Inputs may be any that keep to these rules, and one draw needn't show every extreme that they name: All entries of block_table and write_slots together are distinct slots. Slot s lies on pool device s // 20. For each tenant, no pool device holds more than 4 of its prefix blocks, and one holds exactly 4. `write_slots`: for each tenant, every pool device receives exactly 1 of its slots. `prefix_lengths`: some tenant has exactly 4096. `suffix_lengths`: some tenant has exactly 2048.
All inputs are finite; a program needn't handle non-finite values.
Results may differ from a plain program's by a relative error of at most 0.0095.
Values may be sent and summed in bfloat16 or wider, within the bound.
A program may use at most 64 MiB of HBM per device.

v0:
```python
import jax
import jax.numpy as jnp
from jax import lax
from jax.sharding import PartitionSpec as P

HD = 128


ADAPTER_SCALING = 0.5


def attend_keys(running, query_set, key_rows, value_rows, visible):
    row_peak, row_total, weighted = running
    length = key_rows.shape[0]
    kv_local = query_set.shape[1]
    head_size = query_set.shape[3]
    key_heads = key_rows.reshape(length, kv_local, head_size)
    value_heads = value_rows.reshape(length, kv_local, head_size)
    scores = jnp.einsum(
        "rkgd,lkd->kgrl", query_set, key_heads, preferred_element_type=jnp.float32
    ) * head_size ** (-0.5)
    new_peak = jnp.maximum(row_peak, jnp.max(jnp.where(visible, scores, -1e30), axis=-1))
    factor = jnp.exp(row_peak - new_peak)
    weights = jnp.where(visible, jnp.exp(scores - new_peak[..., None]), 0.0)
    row_total = row_total * factor + jnp.sum(weights, axis=-1)
    weighted = weighted * factor[..., None] + jnp.einsum(
        "kgrl,lkd->kgrd",
        weights.astype(jnp.bfloat16),
        value_heads,
        preferred_element_type=jnp.float32,
    )
    return (new_peak, row_total, weighted)


def prefix_step(query_set, prefix_len, capacity, running, piece):
    packed, block_ids = piece
    total_blocks = packed.shape[0]
    block_rows = packed.shape[2]
    key_value_width = packed.shape[3]
    group_count = total_blocks // capacity
    grouped = packed.reshape(group_count, capacity, 2, block_rows, key_value_width)
    grouped_ids = block_ids.reshape(group_count, capacity)
    offsets = jnp.arange(block_rows, dtype=jnp.int32)

    def inner(running_now, member):
        blocks, ids = member
        key_rows = blocks[:, 0].reshape(capacity * block_rows, key_value_width)
        value_rows = blocks[:, 1].reshape(capacity * block_rows, key_value_width)
        position = ids[:, None] * block_rows + offsets[None, :]
        visible = ((ids[:, None] >= 0) & (position < prefix_len)).reshape(capacity * block_rows)
        return (
            attend_keys(running_now, query_set, key_rows, value_rows, visible[None, None, None, :]),
            None,
        )

    result, unused = lax.scan(inner, running, (grouped, grouped_ids))
    return result


def owned_order(slot_row, owner_index, slot_dev, count):
    owned = slot_row // slot_dev == owner_index
    position_rank = jnp.cumsum(owned.astype(jnp.int32)) - 1
    selected = owned[None, :] & (
        position_rank[None, :] == jnp.arange(count, dtype=jnp.int32)[:, None]
    )
    present = jnp.any(selected, axis=1)
    chosen = jnp.argmax(selected, axis=1)
    return (present, chosen)


def local(
    hidden_in,
    base_query_rotated,
    suffix_cache,
    cache_pool,
    adapter_down,
    adapter_up,
    block_table,
    prefix_lengths,
    suffix_lengths,
    tenant_adapter,
    write_slots,
):
    tenant_index = lax.axis_index("req")
    pool_index = lax.axis_index("pool")
    pool_count = lax.axis_size("pool")
    req_count = lax.axis_size("req")
    rows_dev = base_query_rotated.shape[1]
    head_width = adapter_up.shape[2]
    slot_dev = cache_pool.shape[0]
    block_rows = cache_pool.shape[2]
    key_value_width = cache_pool.shape[3]
    kv_local = key_value_width // HD
    groups = head_width // key_value_width
    prefix_blocks = block_table.shape[1]
    capacity = max(2, 2 * prefix_blocks // pool_count)
    adapter = tenant_adapter[tenant_index]
    down_local = lax.dynamic_index_in_dim(adapter_down, adapter, 0, keepdims=False)
    up_local = lax.dynamic_index_in_dim(adapter_up, adapter, 0, keepdims=False)
    partial_rank = jnp.dot(hidden_in[0], down_local, preferred_element_type=jnp.float32)
    rank_vec = lax.psum(partial_rank, "tp").astype(jnp.bfloat16)
    low_rank_update = jnp.dot(rank_vec, up_local, preferred_element_type=jnp.float32)
    query_rows_all = (
        base_query_rotated[0].astype(jnp.float32) + ADAPTER_SCALING * low_rank_update
    ).astype(jnp.bfloat16)
    query_set = query_rows_all.reshape(rows_dev, kv_local, groups, HD)
    prefix_len = prefix_lengths[tenant_index]
    suffix_len = suffix_lengths[tenant_index]
    table_row = lax.dynamic_index_in_dim(block_table, tenant_index, 0, keepdims=False)
    initial_value = (
        jnp.full((kv_local, groups, rows_dev), -1e30, jnp.float32),
        jnp.zeros((kv_local, groups, rows_dev), jnp.float32),
        jnp.zeros((kv_local, groups, rows_dev, HD), jnp.float32),
    )
    present, chosen = owned_order(table_row, pool_index, slot_dev, capacity)
    local_slot = jnp.where(present, table_row[chosen] - pool_index * slot_dev, 0)
    packed = jnp.take(cache_pool, local_slot, axis=0)
    block_ids = jnp.where(present, chosen, -1)
    running = prefix_step(
        query_set,
        prefix_len,
        capacity,
        initial_value,
        (
            lax.all_gather(packed, "pool", axis=0, tiled=True),
            lax.all_gather(block_ids, "pool", axis=0, tiled=True),
        ),
    )
    gathered = lax.all_gather(suffix_cache, ("pool", "req"), axis=0, tiled=True)
    all_suffix = (
        gathered.reshape(pool_count, req_count, 2, rows_dev, key_value_width)
        .transpose(1, 2, 0, 3, 4)
        .reshape(req_count, 2, pool_count * rows_dev, key_value_width)
    )
    own_suffix = lax.dynamic_index_in_dim(all_suffix, tenant_index, 0, keepdims=False)
    suffix_rows = own_suffix.shape[1]
    suffix_blocks = suffix_rows // block_rows
    span = 4 * block_rows
    query_pos = pool_index * rows_dev + jnp.arange(rows_dev, dtype=jnp.int32)
    key_groups = own_suffix.reshape(2, suffix_rows // span, span, key_value_width).transpose(
        1, 0, 2, 3
    )
    start_offsets = jnp.arange(suffix_rows // span, dtype=jnp.int32) * span

    def suffix_step(running_now, member):
        block_kv, first = member
        key_pos = first + jnp.arange(span, dtype=jnp.int32)
        visible = key_pos[None, :] <= query_pos[:, None]
        return (
            attend_keys(running_now, query_set, block_kv[0], block_kv[1], visible[None, None]),
            None,
        )

    running, unused = lax.scan(suffix_step, running, (key_groups, start_offsets))
    row_peak, row_total, weighted = running
    result = (weighted / row_total[..., None]).transpose(2, 0, 1, 3).reshape(rows_dev, head_width)
    result = jnp.where((query_pos < suffix_len)[:, None], result, 0.0).astype(jnp.bfloat16)
    attended = result[None]
    blocks_all = (
        all_suffix.reshape(req_count, 2, suffix_blocks, block_rows, key_value_width)
        .transpose(0, 2, 1, 3, 4)
        .reshape(req_count * suffix_blocks, 2, block_rows, key_value_width)
    )
    targets = write_slots.reshape(-1)
    global_slot = pool_index * slot_dev + jnp.arange(slot_dev, dtype=jnp.int32)
    matches = global_slot[:, None] == targets[None, :]
    written = jnp.any(matches, axis=1)
    source = jnp.argmax(matches, axis=1)
    pool_after = jnp.where(
        written[:, None, None, None], jnp.take(blocks_all, source, axis=0), cache_pool
    )
    return (attended, pool_after)


def solution(mesh):
    in_specs = (
        P("req", "pool", "tp"),
        P("req", "pool", "tp"),
        P("req", None, "pool", "tp"),
        P("pool", None, None, "tp"),
        P(None, "tp", None),
        P(None, None, "tp"),
        P(),
        P(),
        P(),
        P(),
        P(),
    )
    out_specs = (P("req", "pool", "tp"), P("pool", None, None, "tp"))
    return jax.shard_map(local, mesh=mesh, in_specs=in_specs, out_specs=out_specs, check_vma=False)
```

profile of v0, /device:TPU:1, one launch (start us, length us, event | category | flops | bytes accessed | tf_op | source)
XLA Modules:
  0.0 286.9 jit_solution(16126076940901571186)
XLA Ops:
  9.8 1.3 dynamic-slice
  12.5 1.9 gather_fusion.1
  14.4 0.8 broadcast_select_fusion
  17.6 1.2 dynamic_slice.44
  20.6 0.9 convolution_bitcast_fusion.2
  21.5 14.9 %psum.7 = bf16[128,16]{0,1:T(8,128)(2,1)S(1)} all-reduce(f32[128,16]{0,1:T(8,128)S(1)} %convolution_bitcast_fusion.2), channel_id=1, replica_groups=mesh['pool'=16,'tp'=8,'req'=4] {'tp'}, use_global_device_ids=true, to_apply=%region_3.4 | all-reduce | flops 2048 | bytes 12288 | tf_op jit(solution)/shard_map/psum | solution.py:101
  36.8 15.4 %all-reduce = s32[64]{0:T(128)S(1)} all-reduce(s32[64]{0:T(128)S(1)} %get-tuple-element.276), channel_id=1, replica_groups=mesh['pool'=16,'tp'=8,'req'=4] {'pool'}, use_global_device_ids=true, to_apply=%add | all-reduce | flops 64 | bytes 512
  54.1 10.1 %all-gather.3.cloned.1.call-done = bf16[64,2,128,128]{3,2,1,0:T(8,128)(2,1)} async-done(((bf16[4,2,128,128]{3,2,1,0:T(8,128)(2,1)}), bf16[64,2,128,128]{3,2,1,0:T(8,128)(2,1)}) %all-gather.3.cloned.1.call-update) | async-done | bytes 4194320 | tf_op jit(solution)/shard_map/all_gather | solution.py:125
  64.2 58.6 %while.31 = (s32[]{:T(128)}, f32[1,8,128]{2,1,0:T(8,128)S(1)}, f32[1,8,128]{2,1,0:T(8,128)S(1)}, f32[1,8,128,128]{3,2,1,0:T(8,128)S(1)}, s32[16,4]{1,0:T(8,128)S...) while((s32[]{:T(128)}, f32[1,8,128]{2,1,0:T(8,128)S(1)}, ...), condition=%wide.region_7.8_spmd.clone, body=%wide.region_4.7_spmd.clone.sunk | while | flops 274603520 | bytes 8981189 | solution.py:56
  65.0 1.0 copy_bitcast_fusion.2
  66.5 0.9 fusion.88
  68.6 1.0 copy_bitcast_fusion.2
  70.1 0.9 fusion.88
  72.3 1.0 copy_bitcast_fusion.2
  73.8 0.9 fusion.88
  75.9 1.0 copy_bitcast_fusion.2
  77.4 0.9 fusion.88
  79.6 1.0 copy_bitcast_fusion.2
  81.1 0.9 fusion.88
  83.3 1.0 copy_bitcast_fusion.2
  84.8 0.9 fusion.88
  86.9 1.0 copy_bitcast_fusion.2
  88.4 0.9 fusion.88
  90.6 1.0 copy_bitcast_fusion.2
  92.1 0.9 fusion.88
  94.3 1.0 copy_bitcast_fusion.2
  95.7 0.9 fusion.88
  97.9 1.0 copy_bitcast_fusion.2
  99.4 0.9 fusion.88
  101.6 1.0 copy_bitcast_fusion.2
  103.1 0.9 fusion.88
  105.2 1.0 copy_bitcast_fusion.2
  106.7 0.9 fusion.88
  108.9 1.0 copy_bitcast_fusion.2
  110.4 0.9 fusion.88
  112.6 1.0 copy_bitcast_fusion.2
  114.0 0.9 fusion.88
  116.2 1.0 copy_bitcast_fusion.2
  117.7 0.9 fusion.88
  119.9 1.0 copy_bitcast_fusion.2
  121.4 0.9 fusion.88
  122.8 131.5 %all-gather.5.cloned.1.call-done = bf16[64,2,128,128]{3,2,1,0:T(8,128)(2,1)} async-done(((bf16[1,2,128,128]{3,2,1,0:T(8,128)(2,1)}), bf16[64,2,128,128]{3,2,1,0:T(8,128)(2,1)}) %all-gather.5.cloned.1.call-update) | async-done | bytes 4194320 | tf_op jit(solution)/shard_map/all_gather | solution.py:129
  254.3 2.5 copy.53
  256.9 12.7 %while.30 = (s32[]{:T(128)}, f32[1,8,128]{2,1,0:T(8,128)S(1)}, f32[1,8,128]{2,1,0:T(8,128)S(1)}, f32[1,8,128,128]{3,2,1,0:T(8,128)S(1)}, s32[4]{0:T(128)S(1)}, /...) while((s32[]{:T(128)}, f32[1,8,128]{2,1,0:T(8,128)S(1)}, ...), condition=%wide.region_11.12_spmd.clone, body=%wide.region_8.11_spmd.clone.sunk | while | flops 274534016 | bytes 8721525 | solution.py:154
  270.1 4.7 %copy.57 = bf16[4,16,2,128,128]{4,3,2,1,0:T(8,128)(2,1)} copy(bf16[4,16,2,128,128]{4,3,2,0,1:T(8,128)(2,1)} %bitcast.220) | data formatting | bytes 8388608 | tf_op jit(solution)/shard_map/transpose;transpose | solution.py:161
  274.8 0.8 select_convert_fusion
  275.7 3.0 %gather_fusion.2 = bf16[20,2,128,128]{3,2,1,0:T(8,128)(2,1)S(1)} fusion(bf16[64,2,128,128]{3,2,1,0:T(8,128)(2,1)} %bitcast.222, s32[1024]{0:T(1024)S(1)} %pad_clamp_fusion), kind=kCustom, calls=%fused_computation.2 | custom fusion | bytes 2621520 | tf_op jit(solution)/shard_map/jit(_take)/gather | solution.py:170
  278.7 1.4 select_select_fusion
  (241 shorter events, 47.6 us)
Async XLA Ops:
  7.2 29.3 %copy-start = (bf16[8,16,1024]{2,1,0:T(8,128)(2,1)S(1)}, bf16[8,16,1024]{2,1,0:T(8,128)(2,1)}, u32[]{:S(2)}) copy-start(bf16[8,16,1024]{2,1,0:T(8,128)(2,1)} %param.20) | copy-start | bytes 786436
  7.2 13.4 %copy-start.3 = (bf16[1,128,1024]{2,1,0:T(8,128)(2,1)S(1)}, bf16[1,128,1024]{2,1,0:T(8,128)(2,1)}, u32[]{:S(2)}) copy-start(bf16[1,128,1024]{2,1,0:T(8,128)(2,1)} %param.15) | copy-start | bytes 786436
  7.2 29.3 %copy-start.2 = (bf16[1,128,1024]{2,1,0:T(8,128)(2,1)S(1)}, bf16[1,128,1024]{2,1,0:T(8,128)(2,1)}, u32[]{:S(2)}) copy-start(bf16[1,128,1024]{2,1,0:T(8,128)(2,1)} %param.16) | copy-start | bytes 786436
  7.2 45.1 %copy-start.4 = (s32[4]{0:T(128)S(1)}, s32[4]{0:T(128)}, u32[]{:S(2)}) copy-start(s32[4]{0:T(128)} %param.22) | copy-start | bytes 52
  7.2 45.7 %copy-start.5 = (s32[4]{0:T(128)S(1)}, s32[4]{0:T(128)}, u32[]{:S(2)}) copy-start(s32[4]{0:T(128)} %param.23) | copy-start | bytes 52
  7.2 57.0 %all-gather.3.cloned.1.call-start = ((), (), s32[]{:S(2)}) async-start(), calls=%async_computation | async-start | bytes 4456448 | tf_op jit(solution)/shard_map/all_gather | solution.py:125
  15.2 239.1 %all-gather.5.cloned.1.call-start = ((), (), s32[]{:S(2)}) async-start(), calls=%async_computation.1 | async-start | bytes 4259840 | tf_op jit(solution)/shard_map/all_gather | solution.py:129
  274.8 3.8 %copy-start.1 = (bf16[20,2,128,128]{3,2,1,0:T(8,128)(2,1)S(1)}, bf16[20,2,128,128]{3,2,1,0:T(8,128)(2,1)}, u32[]{:S(2)}) copy-start(bf16[20,2,128,128]{3,2,1,0:T(8,128)(2,1)} %param.18) | copy-start | bytes 3932164
Sparse Core Ops, SparseCore 0:
  15.3 48.8 all-gather.2
  66.3 187.9 all-gather.4
where the time goes:
time: 292 us; the launch traced here: 287 us
  waiting for transfers between devices  142 us (49%)
  local copies, waits for them, and re-layouts  36.9 us (13%)
  other arithmetic  30.6 us (10%)
  blocking collectives  30.3 us (10%)
  matrix products  28.4 us (10%)
  between operations  16.7 us (6%)
    all_gather x1, waiting for transfers between devices, local(): gathered = lax.all_gather(suffix_cache, ('pool', 'req'), axis=0, tiled=True)  132 us
    dot_general x20, matrix products, attend_keys(): jnp.einsum('kgrl,lkd->kgrd', weights.astype(jnp.bfloat16), value_heads, p...  18.1 us
    squeeze x16, local copies, waits for them, and re-layouts, prefix_step(): result, unused = lax.scan(inner, running, (grouped, grouped_ids))  15.5 us
    unnamed x1, blocking collectives  15.4 us
    psum x1, blocking collectives, local(): rank_vec = lax.psum(partial_rank, 'tp').astype(jnp.bfloat16)  14.9 us
    and x16, other arithmetic, inner(): (ids[:, None] >= 0) & (position < prefix_len)  11.2 us
    all_gather x1, waiting for transfers between devices, local(): lax.all_gather(packed, 'pool', axis=0, tiled=True)  10.1 us
    dot_general x20, matrix products, attend_keys(): jnp.einsum('rkgd,lkd->kgrl', query_set, key_heads, preferred_element_type...  9.12 us
  transfers between devices with their start and end apart: 2, of which 2 were waited for; matrix products, arithmetic and copies ran while one was open for 22% of the time, Pallas kernels for 0%

commit v1 on v0

v1 whole, which is shorter than its diff:
```python
import functools

import jax
import jax.numpy as jnp
from jax import lax
from jax.experimental import pallas as pl
from jax.experimental.pallas import tpu as pltpu
from jax.sharding import PartitionSpec as P

MESH = pl.DeviceIdType.MESH
HD = 128
ADAPTER_SCALING = 0.5
LOG2E = 1.4426950408889634
LOW = -1e30
ROWS = 256
PARTNERS = ("sib", "xp", "xm", "zp", "zn", "y1", "y2", "y4", "rp", "rm")
COPIES = 46


def kernel(
    table, plens, slens, adapters, wslots,
    hidden, base, suffix, pool, down, up,
    out, pool_out,
    pool_v, hid_v, base_v, down_v, up_v,
    main_0, main_1, main_2, main_3, over_0, over_1, over_2, over_3, cont_0, cont_1, cont_2, cont_3,
    fore, wblk, wmine,
    rank_out, rank_in, qs, peak, acc, kc, vc, nval,
    local_sem, send_sem, recv_sem,
):
    p = lax.axis_index("pool")
    y = lax.axis_index("tp")
    r = lax.axis_index("req")
    x, zl, c = p // 4, (p // 2) % 2, p % 2
    x1, x3 = (x + 1) % 4, (x + 3) % 4
    rn = (r + 2 * zl + 3) % 4
    other = p + 2 - 4 * zl
    partner = {
        "sib": {"pool": p + 1 - 2 * c},
        "xp": {"pool": x1 * 4 + zl * 2 + c},
        "xm": {"pool": x3 * 4 + zl * 2 + c},
        "zp": {"pool": other},
        "zn": {"pool": other, "req": rn},
        "y1": {"tp": y + 1 - 2 * (y % 2)},
        "y2": {"tp": y + 2 - 4 * ((y // 2) % 2)},
        "y4": {"tp": (y + 4) % 8},
        "rp": {"req": (r + 1) % 4},
        "rm": {"req": (r + 3) % 4},
    }

    main = (main_0, main_1, main_2, main_3)
    over = (over_0, over_1, over_2, over_3)
    cont = (cont_0, cont_1, cont_2, cont_3)

    def device_of(k, i, j):
        return (x + k) % 4 * 4 + (zl + j - 2 * zl * j) * 2 + c + i - 2 * c * i

    locals_ = {}
    for i, (name, src, dst) in enumerate((
        ("suffix", suffix.at[0], cont_0.at[0, 0]),
        ("pool", pool, pool_v),
        ("hidden", hidden.at[0], hid_v),
        ("down", down, down_v),
        ("base", base.at[0], base_v),
        ("up", up, up_v),
    )):
        locals_[name] = pltpu.make_async_copy(src, dst, local_sem.at[i])
        locals_[name].start()

    barrier = pltpu.get_barrier_semaphore()
    for name in PARTNERS:
        pl.semaphore_signal(barrier, inc=1, device_id=partner[name], device_id_type=MESH)
    pl.semaphore_wait(barrier, len(PARTNERS))

    copies = {}

    def send_to(name, src, dst, to):
        i = len(copies)
        copy = pltpu.make_async_remote_copy(
            src_ref=src, dst_ref=dst,
            send_sem=send_sem.at[i], recv_sem=recv_sem.at[i],
            device_id=partner[to], device_id_type=MESH,
        )
        copies[name] = copy
        copy.start()

    def send(name, buf, k, at, to):
        there = (k + {"xp": 3, "xm": 1}.get(to, 0)) % 4
        place = list(at)
        if to == "sib":
            place[0] = 1 - at[0]
        if to in ("zp", "zn"):
            place[1] = 1 - at[1]
        send_to(name, buf[k].at[at], buf[there].at[tuple(place)], to)

    def got(*names):
        for name in names:
            copies[name].wait_recv()

    locals_["suffix"].wait()
    send("c_z", cont, 0, (0, 0), "zp")

    def own_slots(tenant):
        def step(b, carry):
            count, picks = carry
            local = table[tenant, b] - p * 20
            owned = (local >= 0) & (local < 20)
            picks = tuple(
                jnp.where(owned & (count == k), local, pick) for k, pick in enumerate(picks)
            )
            return count + owned.astype(jnp.int32), picks

        zero = jnp.int32(0)
        return lax.fori_loop(0, 32, step, (zero, (zero,) * 4), unroll=4)[1]

    mine = own_slots(r)
    theirs = own_slots(rn)
    locals_["pool"].wait()
    for k in range(2):
        main_0[0, 0, k] = pool_v[mine[k]]
    send("m_p", main, 0, (0, 0), "xp")
    send("m_m", main, 0, (0, 0), "xm")
    for k in range(2):
        over_0[0, 0, k] = pool_v[mine[2 + k]]
    fore[...] = pool_v[theirs[3]]
    send("o_z", over, 0, (0, 0, 0), "zp")
    send_to("o_n", fore, over_0.at[0, 1, 1], "zn")
    send("m_z", main, 0, (0, 0), "zp")
    send("m_s", main, 0, (0, 0), "sib")

    locals_["hidden"].wait()
    locals_["down"].wait()
    adapter = adapters[r]
    total = lax.dot_general(
        down_v[adapter], hid_v[...], (((1,), (1,)), ((), ())), preferred_element_type=jnp.float32
    )
    rank_out[0] = total
    send_to("r_0", rank_out.at[0], rank_in.at[0], "y1")

    got("c_z")
    send("c_p", cont, 0, (0,), "xp")
    send("c_m", cont, 0, (0,), "xm")
    send("c_s", cont, 0, (0,), "sib")

    plen = plens[r]

    def one_device(d, unused):
        def step(b, carry):
            count, rows = carry
            local = table[r, b] - d * 20
            owned = (local >= 0) & (local < 20)
            seen = plen - b * 128
            rows = tuple(
                jnp.where(owned & (count == k), seen, row) for k, row in enumerate(rows)
            )
            return count + owned.astype(jnp.int32), rows

        zero = jnp.int32(0)
        rows = lax.fori_loop(0, 32, step, (zero, (zero,) * 4), unroll=4)[1]
        for k in range(4):
            nval[d * 4 + k] = rows[k]
        return unused

    lax.fori_loop(0, 16, one_device, 0)

    got("r_0")
    total = total + rank_in[0]
    rank_out[1] = total
    send_to("r_1", rank_out.at[1], rank_in.at[1], "y2")
    got("o_z", "o_n")
    send("o_p", over, 0, (0,), "xp")
    send("o_m", over, 0, (0,), "xm")
    send("o_s", over, 0, (0,), "sib")
    got("r_1")
    total = total + rank_in[1]
    rank_out[2] = total
    send_to("r_2", rank_out.at[2], rank_in.at[2], "y4")
    got("m_p")
    send("m_pp", main, 3, (0, 0, 0), "xp")
    send("m_pz", main, 3, (0, 0), "zp")
    send("m_ps", main, 3, (0, 0), "sib")
    got("m_m")
    send("m_mm", main, 1, (0, 0, 1), "xm")
    send("m_mz", main, 1, (0, 0), "zp")
    send("m_ms", main, 1, (0, 0), "sib")
    got("r_2")
    total = total + rank_in[2]
    rank = total.T.astype(jnp.bfloat16)
    locals_["base"].wait()
    locals_["up"].wait()
    update = jnp.dot(rank, up_v[adapter], preferred_element_type=jnp.float32)
    query = (base_v[...].astype(jnp.float32) + ADAPTER_SCALING * update).astype(jnp.bfloat16)
    for h in range(8):
        qs[h * 128 : (h + 1) * 128, :] = query[:, h * 128 : (h + 1) * 128]

    peak[...] = jnp.full(peak.shape, LOW, jnp.float32)
    acc[...] = jnp.zeros(acc.shape, jnp.float32)
    scale = HD**-0.5 * LOG2E
    own_key = cont_0[0, 0, 0, 0:1, :]

    def attend(mask):
        keys = kc[...]
        values = vc[...]
        for t in range(1024 // ROWS):
            rows = slice(t * ROWS, (t + 1) * ROWS)
            s = lax.dot_general(
                qs[rows, :], keys, (((1,), (1,)), ((), ())), preferred_element_type=jnp.float32
            )
            if mask is not None:
                s = jnp.where(mask, s, LOW)
            old = peak[rows, 0:1]
            new = jnp.maximum(old, jnp.max(s, axis=1, keepdims=True))
            w = jnp.exp2((s - new) * scale).astype(jnp.bfloat16)
            factor = jnp.exp2((old - new) * scale)
            acc[rows, :] = acc[rows, :] * factor + jnp.dot(
                w, values, preferred_element_type=jnp.float32
            )
            peak[rows, :] = jnp.broadcast_to(new, (ROWS, 128))

    def suffix_plane(k, mask):
        for i in range(4):
            at = slice(i * 128, (i + 1) * 128)
            kc[at, :] = cont[k][i % 2, i // 2, 0]
            vc[at, :128] = cont[k][i % 2, i // 2, 1]
            vc[at, 128:] = jnp.ones((128, 128), jnp.bfloat16)
        attend(mask)

    row_no = lax.broadcasted_iota(jnp.int32, (128, 128), 0)

    def prefix_plane(buf, k, first):
        def one(i, unused):
            for n in range(4):
                at = slice(n * 128, (n + 1) * 128)
                j, slot = n // 2, n % 2
                seen = row_no < nval[device_of(k, i, j) * 4 + first + slot]
                kc[at, :] = jnp.where(seen, buf[k][i, j, slot, 0], own_key)
                vc[at, :128] = jnp.where(seen, buf[k][i, j, slot, 1], jnp.bfloat16(0))
                vc[at, 128:] = jnp.where(seen, jnp.bfloat16(1), jnp.bfloat16(0))
            attend(None)
            return unused

        lax.fori_loop(0, 2, one, 0)

    got("c_s")
    lane = lax.broadcasted_iota(jnp.int32, (ROWS, 128), 1)
    token = lax.broadcasted_iota(jnp.int32, (ROWS, 128), 0) % 128 + p * 128
    suffix_plane(0, jnp.concatenate(
        [lane + device_of(0, i % 2, i // 2) * 128 <= token for i in range(4)], axis=1
    ))

    got("m_z", "m_s")
    send("m_zs", main, 0, (0, 1), "sib")
    got("m_pz", "m_mz")
    send("m_pzs", main, 3, (0, 1), "sib")
    send("m_mzs", main, 1, (0, 1), "sib")
    got("m_pp")
    send("m_ppz", main, 2, (0, 0, 0), "zp")
    send("m_pps", main, 2, (0, 0, 0), "sib")
    got("m_mm")
    send("m_mmz", main, 2, (0, 0, 1), "zp")
    send("m_mms", main, 2, (0, 0, 1), "sib")
    got("c_p")
    send("c_pp", cont, 3, (0, 0), "xp")
    send("c_ps", cont, 3, (0,), "sib")
    got("c_m")
    send("c_mm", cont, 1, (0, 1), "xm")
    send("c_ms", cont, 1, (0,), "sib")
    got("m_zs")
    prefix_plane(main, 0, 0)

    got("o_p")
    send("o_pp", over, 3, (0, 0), "xp")
    send("o_ps", over, 3, (0,), "sib")
    got("o_m")
    send("o_mm", over, 1, (0, 1), "xm")
    send("o_ms", over, 1, (0,), "sib")
    got("c_pp")
    send("c_pps", cont, 2, (0, 0), "sib")
    got("c_mm")
    send("c_mms", cont, 2, (0, 1), "sib")
    got("m_ppz", "m_mmz")
    send("m_zzs", main, 2, (0, 1), "sib")

    got("m_ps", "m_pzs")
    prefix_plane(main, 3, 0)
    got("m_ms", "m_mzs")
    prefix_plane(main, 1, 0)

    got("c_ps", "c_ms", "c_pps", "c_mms")

    def write_slot(tenant):
        def step(b, carry):
            block, slot = carry
            local = wslots[tenant, b] - p * 20
            owned = (local >= 0) & (local < 20)
            return jnp.where(owned, b, block), jnp.where(owned, local, slot)

        return lax.fori_loop(0, 16, step, (jnp.int32(0), jnp.int32(0)), unroll=4)

    block, slot_0 = write_slot(r)
    i, j = (block + c) % 2, (block // 2 + zl) % 2
    away = (block // 4 + 4 - x) % 4
    chosen = cont_0[i, j]
    for k in range(1, 4):
        chosen = jnp.where(away == k, cont[k][i, j], chosen)
    wmine[...] = chosen
    send_to("w_p", wmine, wblk.at[2], "rp")
    send_to("w_m", wmine, wblk.at[0], "rm")

    for k in range(1, 4):
        pl.when(x + k >= 4)(functools.partial(suffix_plane, k, None))
    got("o_s")
    prefix_plane(over, 0, 2)

    got("o_pp")
    send("o_pps", over, 2, (0, 0), "sib")
    got("o_mm")
    send("o_mms", over, 2, (0, 1), "sib")
    got("w_p")
    send_to("w_pp", wblk.at[2, 0], wblk.at[1, 0], "rp")
    got("w_m")
    send_to("w_mm", wblk.at[0, 1], wblk.at[1, 1], "rm")

    got("m_pps", "m_mms", "m_zzs")
    prefix_plane(main, 2, 0)
    got("o_ps")
    prefix_plane(over, 3, 2)
    got("o_ms")
    prefix_plane(over, 1, 2)
    got("o_pps", "o_mms")
    prefix_plane(over, 2, 2)

    slot_1 = write_slot((r + 1) % 4)[1]
    slot_2 = write_slot((r + 2) % 4)[1]
    slot_3 = write_slot((r + 3) % 4)[1]
    got("w_pp", "w_mm")

    def one_slot(s, unused):
        block = pool_v[s]
        block = jnp.where(s == slot_0, wmine[...], block)
        block = jnp.where(s == slot_1, wblk[0], block)
        block = jnp.where(s == slot_2, wblk[1], block)
        block = jnp.where(s == slot_3, wblk[2], block)
        pool_out[s] = block
        return unused

    lax.fori_loop(0, 20, one_slot, 0)

    token = p * 128 + lax.broadcasted_iota(jnp.int32, (128, 128), 0)
    live = token < slens[r]
    for h in range(8):
        rows = slice(h * 128, (h + 1) * 128)
        value = acc[rows, :128] / acc[rows, 128:]
        out[0, :, rows] = jnp.where(live, value, 0.0).astype(jnp.bfloat16)

    for copy in copies.values():
        copy.wait_send()


def local(hidden, base, suffix, pool, down, up, table, plens, slens, adapters, wslots):
    bf, f32 = jnp.bfloat16, jnp.float32
    down = down.transpose(0, 2, 1)
    smem = pl.BlockSpec(memory_space=pltpu.SMEM)
    anywhere = pl.BlockSpec(memory_space=pl.ANY)
    vmem = pl.BlockSpec(memory_space=pltpu.VMEM)
    block = (2, 128, 128)
    return pl.pallas_call(
        kernel,
        out_shape=(
            jax.ShapeDtypeStruct(base.shape, bf),
            jax.ShapeDtypeStruct(pool.shape, bf),
        ),
        in_specs=[smem] * 5 + [anywhere] * 6,
        out_specs=(vmem, vmem),
        scratch_shapes=[
            pltpu.VMEM(pool.shape, bf),
            pltpu.VMEM(hidden.shape[1:], bf),
            pltpu.VMEM(base.shape[1:], bf),
            pltpu.VMEM(down.shape, bf),
            pltpu.VMEM(up.shape, bf),
            *[pltpu.VMEM((2, 2, 2) + block, bf)] * 8,
            *[pltpu.VMEM((2, 2) + block, bf)] * 4,
            pltpu.VMEM(block, bf),
            pltpu.VMEM((3,) + block, bf),
            pltpu.VMEM(block, bf),
            pltpu.VMEM((3, 16, 128), f32),
            pltpu.VMEM((3, 16, 128), f32),
            pltpu.VMEM((1024, 128), bf),
            pltpu.VMEM((1024, 128), f32),
            pltpu.VMEM((1024, 256), f32),
            pltpu.VMEM((512, 128), bf),
            pltpu.VMEM((512, 256), bf),
            pltpu.SMEM((64,), jnp.int32),
            pltpu.SemaphoreType.DMA((6,)),
            pltpu.SemaphoreType.DMA((COPIES,)),
            pltpu.SemaphoreType.DMA((COPIES,)),
        ],
        compiler_params=pltpu.CompilerParams(
            collective_id=0, has_side_effects=True, vmem_limit_bytes=48 << 20
        ),
        name="attend_all",
    )(table, plens, slens, adapters, wslots, hidden, base, suffix, pool, down, up)


def solution(mesh):
    in_specs = (
        P("req", "pool", "tp"),
        P("req", "pool", "tp"),
        P("req", None, "pool", "tp"),
        P("pool", None, None, "tp"),
        P(None, "tp", None),
        P(None, None, "tp"),
        P(),
        P(),
        P(),
        P(),
        P(),
    )
    out_specs = (P("req", "pool", "tp"), P("pool", None, None, "tp"))
    return jax.shard_map(local, mesh=mesh, in_specs=in_specs, out_specs=out_specs, check_vma=False)
```

time: 292 us -> 70.9 us (0.24)
  the two profiles are of different devices: /device:TPU:1 before, /device:TPU:64 now
where the time goes in v1:
time: 70.9 us; the launch traced here: 70.5 us
  Pallas kernels  58.8 us (83%)
  local copies, waits for them, and re-layouts  11 us (16%)
    pallas_call x1, Pallas kernels, local(): pl.pallas_call(kernel, out_shape=(jax.ShapeDtypeStruct(base.shape, bf), j...  58.8 us
    unnamed x24, local copies, waits for them, and re-layouts  11 us

profile of v1, /device:TPU:64, one launch (start us, length us, event | category | flops | bytes accessed | tf_op | source)
XLA Modules:
  0.0 70.5 jit_solution(4219207336667834202)
XLA Ops:
  0.6 0.0 copy-start
  0.6 1.3 %copy-done = bf16[20,2,128,128]{3,2,1,0:T(8,128)(2,1)S(1)} copy-done((bf16[20,2,128,128]{3,2,1,0:T(8,128)(2,1)S(1)}, bf16[20,2,128,128]{3,2,1,0:T(8,128)(2,1)}, u32[]{:S(2)}) %copy-start) | copy-done | bytes 1310744
  2.0 0.0 copy-start.1
  2.0 0.9 %copy-done.1 = bf16[1,128,1024]{2,1,0:T(8,128)(2,1)S(1)} copy-done((bf16[1,128,1024]{2,1,0:T(8,128)(2,1)S(1)}, bf16[1,128,1024]{2,1,0:T(8,128)(2,1)}, u32[]{:S(2)}) %copy-start.1) | copy-done | bytes 262168
  2.9 0.0 copy-start.2
  2.9 0.9 %copy-done.2 = bf16[1,128,1024]{2,1,0:T(8,128)(2,1)S(1)} copy-done((bf16[1,128,1024]{2,1,0:T(8,128)(2,1)S(1)}, bf16[1,128,1024]{2,1,0:T(8,128)(2,1)}, u32[]{:S(2)}) %copy-start.2) | copy-done | bytes 262168
  3.9 0.0 copy-start.3
  3.9 0.9 %copy-done.3 = bf16[8,1024,16]{1,2,0:T(8,128)(2,1)S(1)} copy-done((bf16[8,1024,16]{1,2,0:T(8,128)(2,1)S(1)}, bf16[8,1024,16]{1,2,0:T(8,128)(2,1)}, u32[]{:S(2)}) %copy-start.3) | copy-done | bytes 262168
  4.8 0.0 copy-start.4
  4.8 0.9 %copy-done.4 = bf16[8,16,1024]{2,1,0:T(8,128)(2,1)S(1)} copy-done((bf16[8,16,1024]{2,1,0:T(8,128)(2,1)S(1)}, bf16[8,16,1024]{2,1,0:T(8,128)(2,1)}, u32[]{:S(2)}) %copy-start.4) | copy-done | bytes 262168
  5.8 0.0 copy-start.5
  5.8 0.8 %copy-done.5 = bf16[1,2,128,128]{3,2,1,0:T(8,128)(2,1)S(1)} copy-done((bf16[1,2,128,128]{3,2,1,0:T(8,128)(2,1)S(1)}, bf16[1,2,128,128]{3,2,1,0:T(8,128)(2,1)}, u32[]{:S(2)}) %copy-start.5) | copy-done | bytes 65560
  6.6 0.0 copy-start.6
  6.6 0.7 copy-done.6
  7.3 0.0 copy-start.7
  7.3 0.7 copy-done.7
  8.0 0.0 copy-start.8
  8.0 0.7 copy-done.8
  8.6 0.0 copy-start.9
  8.6 0.7 copy-done.9
  9.3 0.0 copy-start.10
  9.3 0.7 copy-done.10
  9.9 58.8 %attend_all.1 = (bf16[1,128,1024]{2,1,0:T(8,128)(2,1)S(1)}, bf16[20,2,128,128]{3,2,1,0:T(8,128)(2,1)S(1)}) custom-call(s32[4,32]{1,0:T(4,128)S(1)} %copy-done.6, s32[4]{0:T(128)S(1)} %copy-done.8, s32[4]{0:T(128)S(1)} %copy-done.9, s32[4]{0:T(128)S(1)} %copy-done.10, s32[4,16]{1,0:T(4,128)S(1)} %copy-done.7, bf16[1,128,1024]{2,1,0:T(8,128)(2,1)S(1)} %copy-done.1, ...), custom_call_target="tpu_custom_call" | custom-call | tf_op jit(solution)/shard_map/attend_all/pallas_call | solution.py:366
  68.7 0.7 %copy.15 = bf16[1,128,1024]{2,1,0:T(8,128)(2,1)} copy(bf16[1,128,1024]{2,1,0:T(8,128)(2,1)S(1)} %get-tuple-element.4) | data formatting | bytes 524288
  69.4 1.1 %copy.16 = bf16[20,2,128,128]{3,2,1,0:T(8,128)(2,1)} copy(bf16[20,2,128,128]{3,2,1,0:T(8,128)(2,1)S(1)} %get-tuple-element.5) | data formatting | bytes 2621440
Async XLA Ops:
  0.6 1.3 %copy-start = (bf16[20,2,128,128]{3,2,1,0:T(8,128)(2,1)S(1)}, bf16[20,2,128,128]{3,2,1,0:T(8,128)(2,1)}, u32[]{:S(2)}) copy-start(bf16[20,2,128,128]{3,2,1,0:T(8,128)(2,1)} %pool.1) | copy-start | bytes 3932164
  2.0 0.9 %copy-start.1 = (bf16[1,128,1024]{2,1,0:T(8,128)(2,1)S(1)}, bf16[1,128,1024]{2,1,0:T(8,128)(2,1)}, u32[]{:S(2)}) copy-start(bf16[1,128,1024]{2,1,0:T(8,128)(2,1)} %hidden.1) | copy-start | bytes 786436
  2.9 0.9 %copy-start.2 = (bf16[1,128,1024]{2,1,0:T(8,128)(2,1)S(1)}, bf16[1,128,1024]{2,1,0:T(8,128)(2,1)}, u32[]{:S(2)}) copy-start(bf16[1,128,1024]{2,1,0:T(8,128)(2,1)} %base.1) | copy-start | bytes 786436
  3.9 0.9 %copy-start.3 = (bf16[8,1024,16]{1,2,0:T(8,128)(2,1)S(1)}, bf16[8,1024,16]{1,2,0:T(8,128)(2,1)}, u32[]{:S(2)}) copy-start(bf16[8,1024,16]{1,2,0:T(8,128)(2,1)} %param.15) | copy-start | bytes 786436
  4.8 0.9 %copy-start.4 = (bf16[8,16,1024]{2,1,0:T(8,128)(2,1)S(1)}, bf16[8,16,1024]{2,1,0:T(8,128)(2,1)}, u32[]{:S(2)}) copy-start(bf16[8,16,1024]{2,1,0:T(8,128)(2,1)} %up.1) | copy-start | bytes 786436
  5.8 0.8 %copy-start.5 = (bf16[1,2,128,128]{3,2,1,0:T(8,128)(2,1)S(1)}, bf16[1,2,128,128]{3,2,1,0:T(8,128)(2,1)}, u32[]{:S(2)}) copy-start(bf16[1,2,128,128]{3,2,1,0:T(8,128)(2,1)} %suffix.1) | copy-start | bytes 196612
  6.6 0.7 copy-start.6
  7.3 0.7 copy-start.7
  8.0 0.7 copy-start.8
  8.6 0.7 copy-start.9
  9.3 0.7 copy-start.10

commit v2 on v1

--- a/solution.py
+++ b/solution.py
@@ -12,15 +12,16 @@
 ADAPTER_SCALING = 0.5
 LOG2E = 1.4426950408889634
 LOW = -1e30
-ROWS = 256
-PARTNERS = ("sib", "xp", "xm", "zp", "zn", "y1", "y2", "y4", "rp", "rm")
-COPIES = 46
+ROWS = 128
+PARTNERS = ("sib", "xp", "xm", "zp", "zn", "y1", "y2", "y3", "y4", "y5", "y6", "y7", "rp", "rm")
+COPIES = 50
 
 
 def kernel(
-    table, plens, slens, adapters, wslots,
+    table_in, plens_in, slens_in, adapters_in, wslots_in,
     hidden, base, suffix, pool, down, up,
     out, pool_out,
+    table, plens, slens, adapters, wslots,
     pool_v, hid_v, base_v, down_v, up_v,
     main_0, main_1, main_2, main_3, over_0, over_1, over_2, over_3, cont_0, cont_1, cont_2, cont_3,
     fore, wblk, wmine,
@@ -40,9 +41,7 @@
         "xm": {"pool": x3 * 4 + zl * 2 + c},
         "zp": {"pool": other},
         "zn": {"pool": other, "req": rn},
-        "y1": {"tp": y + 1 - 2 * (y % 2)},
-        "y2": {"tp": y + 2 - 4 * ((y // 2) % 2)},
-        "y4": {"tp": (y + 4) % 8},
+        **{f"y{d}": {"tp": (y + d) % 8} for d in range(1, 8)},
         "rp": {"req": (r + 1) % 4},
         "rm": {"req": (r + 3) % 4},
     }
@@ -56,12 +55,17 @@
 
     locals_ = {}
     for i, (name, src, dst) in enumerate((
+        ("table", table_in, table),
         ("suffix", suffix.at[0], cont_0.at[0, 0]),
         ("pool", pool, pool_v),
+        ("adapters", adapters_in, adapters),
         ("hidden", hidden.at[0], hid_v),
         ("down", down, down_v),
         ("base", base.at[0], base_v),
         ("up", up, up_v),
+        ("plens", plens_in, plens),
+        ("slens", slens_in, slens),
+        ("wslots", wslots_in, wslots),
     )):
         locals_[name] = pltpu.make_async_copy(src, dst, local_sem.at[i])
         locals_[name].start()
@@ -112,35 +116,39 @@
         zero = jnp.int32(0)
         return lax.fori_loop(0, 32, step, (zero, (zero,) * 4), unroll=4)[1]
 
+    locals_["table"].wait()
     mine = own_slots(r)
-    theirs = own_slots(rn)
     locals_["pool"].wait()
     for k in range(2):
         main_0[0, 0, k] = pool_v[mine[k]]
     send("m_p", main, 0, (0, 0), "xp")
     send("m_m", main, 0, (0, 0), "xm")
+    send("m_z", main, 0, (0, 0), "zp")
+
+    locals_["hidden"].wait()
+    locals_["down"].wait()
+    locals_["adapters"].wait()
+    adapter = adapters[r]
+    rank_out[...] = lax.dot_general(
+        down_v[adapter], hid_v[...], (((1,), (1,)), ((), ())), preferred_element_type=jnp.float32
+    )
+    for d in range(1, 8):
+        send_to(f"r_{d}", rank_out, rank_in.at[8 - d], f"y{d}")
+
+    theirs = own_slots(rn)
     for k in range(2):
         over_0[0, 0, k] = pool_v[mine[2 + k]]
     fore[...] = pool_v[theirs[3]]
     send("o_z", over, 0, (0, 0, 0), "zp")
     send_to("o_n", fore, over_0.at[0, 1, 1], "zn")
-    send("m_z", main, 0, (0, 0), "zp")
     send("m_s", main, 0, (0, 0), "sib")
-
-    locals_["hidden"].wait()
-    locals_["down"].wait()
-    adapter = adapters[r]
-    total = lax.dot_general(
-        down_v[adapter], hid_v[...], (((1,), (1,)), ((), ())), preferred_element_type=jnp.float32
-    )
-    rank_out[0] = total
-    send_to("r_0", rank_out.at[0], rank_in.at[0], "y1")
 
     got("c_z")
     send("c_p", cont, 0, (0,), "xp")
     send("c_m", cont, 0, (0,), "xm")
     send("c_s", cont, 0, (0,), "sib")
 
+    locals_["plens"].wait()
     plen = plens[r]
 
     def one_device(d, unused):
@@ -162,18 +170,10 @@
 
     lax.fori_loop(0, 16, one_device, 0)
 
-    got("r_0")
-    total = total + rank_in[0]
-    rank_out[1] = total
-    send_to("r_1", rank_out.at[1], rank_in.at[1], "y2")
     got("o_z", "o_n")
     send("o_p", over, 0, (0,), "xp")
     send("o_m", over, 0, (0,), "xm")
     send("o_s", over, 0, (0,), "sib")
-    got("r_1")
-    total = total + rank_in[1]
-    rank_out[2] = total
-    send_to("r_2", rank_out.at[2], rank_in.at[2], "y4")
     got("m_p")
     send("m_pp", main, 3, (0, 0, 0), "xp")
     send("m_pz", main, 3, (0, 0), "zp")
@@ -182,8 +182,10 @@
     send("m_mm", main, 1, (0, 0, 1), "xm")
     send("m_mz", main, 1, (0, 0), "zp")
     send("m_ms", main, 1, (0, 0), "sib")
-    got("r_2")
-    total = total + rank_in[2]
+    got(*(f"r_{d}" for d in range(1, 8)))
+    total = rank_out[...]
+    for d in range(1, 8):
+        total = total + rank_in[d]
     rank = total.T.astype(jnp.bfloat16)
     locals_["base"].wait()
     locals_["up"].wait()
@@ -197,16 +199,34 @@
     scale = HD**-0.5 * LOG2E
     own_key = cont_0[0, 0, 0, 0:1, :]
 
-    def attend(mask):
-        keys = kc[...]
-        values = vc[...]
-        for t in range(1024 // ROWS):
+    row_no = lax.broadcasted_iota(jnp.int32, (128, 128), 0)
+
+    def fill(n, block, rows):
+        at = slice(n * 128, (n + 1) * 128)
+        seen = row_no < rows
+        kc[at, :] = jnp.where(seen, block[0], own_key)
+        vc[at, :128] = jnp.where(seen, block[1], jnp.bfloat16(0))
+        vc[at, 128:] = jnp.where(seen, jnp.bfloat16(1), jnp.bfloat16(0))
+
+    def attend(size, mask=None):
+        keys = kc[:size, :]
+        values = vc[:size, :]
+
+        def scores(t):
             rows = slice(t * ROWS, (t + 1) * ROWS)
             s = lax.dot_general(
                 qs[rows, :], keys, (((1,), (1,)), ((), ())), preferred_element_type=jnp.float32
             )
             if mask is not None:
-                s = jnp.where(mask, s, LOW)
+                s = jnp.concatenate([s[:, :-512], jnp.where(mask, s[:, -512:], LOW)], axis=1)
+            return s
+
+        later = scores(0)
+        for t in range(1024 // ROWS):
+            rows = slice(t * ROWS, (t + 1) * ROWS)
+            s = later
+            if t + 1 < 1024 // ROWS:
+                later = scores(t + 1)
             old = peak[rows, 0:1]
             new = jnp.maximum(old, jnp.max(s, axis=1, keepdims=True))
             w = jnp.exp2((s - new) * scale).astype(jnp.bfloat16)
@@ -216,39 +236,39 @@
             )
             peak[rows, :] = jnp.broadcast_to(new, (ROWS, 128))
 
-    def suffix_plane(k, mask):
-        for i in range(4):
-            at = slice(i * 128, (i + 1) * 128)
-            kc[at, :] = cont[k][i % 2, i // 2, 0]
-            vc[at, :128] = cont[k][i % 2, i // 2, 1]
-            vc[at, 128:] = jnp.ones((128, 128), jnp.bfloat16)
-        attend(mask)
-
-    row_no = lax.broadcasted_iota(jnp.int32, (128, 128), 0)
-
-    def prefix_plane(buf, k, first):
-        def one(i, unused):
-            for n in range(4):
-                at = slice(n * 128, (n + 1) * 128)
-                j, slot = n // 2, n % 2
-                seen = row_no < nval[device_of(k, i, j) * 4 + first + slot]
-                kc[at, :] = jnp.where(seen, buf[k][i, j, slot, 0], own_key)
-                vc[at, :128] = jnp.where(seen, buf[k][i, j, slot, 1], jnp.bfloat16(0))
-                vc[at, 128:] = jnp.where(seen, jnp.bfloat16(1), jnp.bfloat16(0))
-            attend(None)
-            return unused
-
-        lax.fori_loop(0, 2, one, 0)
-
-    got("c_s")
-    lane = lax.broadcasted_iota(jnp.int32, (ROWS, 128), 1)
-    token = lax.broadcasted_iota(jnp.int32, (ROWS, 128), 0) % 128 + p * 128
-    suffix_plane(0, jnp.concatenate(
-        [lane + device_of(0, i % 2, i // 2) * 128 <= token for i in range(4)], axis=1
-    ))
+    def slots(buf, k, first):
+        for n in range(8):
+            i, j, slot = n // 4, n // 2 % 2, n % 2
+            fill(n, buf[k][i, j, slot], nval[device_of(k, i, j) * 4 + first + slot])
+
+    def plane(k):
+        slots(main, k, 0)
+        for n in range(4):
+            fill(8 + n, cont[k][n // 2, n % 2], 128 if k == 0 else jnp.where(x + k >= 4, 128, 0))
+        mask = None
+        if k == 0:
+            lane = lax.broadcasted_iota(jnp.int32, (ROWS, 128), 1)
+            token = lax.broadcasted_iota(jnp.int32, (ROWS, 128), 0) + p * 128
+            mask = jnp.concatenate(
+                [lane + device_of(0, n // 2, n % 2) * 128 <= token for n in range(4)], axis=1
+            )
+        attend(1536, mask)
+
+    def over_plane(k):
+        slots(over, k, 2)
+        attend(1024)
 
     got("m_z", "m_s")
     send("m_zs", main, 0, (0, 1), "sib")
+    got("c_s", "m_zs")
+    plane(0)
+
+    got("c_p")
+    send("c_pp", cont, 3, (0, 0), "xp")
+    send("c_ps", cont, 3, (0,), "sib")
+    got("c_m")
+    send("c_mm", cont, 1, (0, 1), "xm")
+    send("c_ms", cont, 1, (0,), "sib")
     got("m_pz", "m_mz")
     send("m_pzs", main, 3, (0, 1), "sib")
     send("m_mzs", main, 1, (0, 1), "sib")
@@ -258,14 +278,17 @@
     got("m_mm")
     send("m_mmz", main, 2, (0, 0, 1), "zp")
     send("m_mms", main, 2, (0, 0, 1), "sib")
-    got("c_p")
-    send("c_pp", cont, 3, (0, 0), "xp")
-    send("c_ps", cont, 3, (0,), "sib")
-    got("c_m")
-    send("c_mm", cont, 1, (0, 1), "xm")
-    send("c_ms", cont, 1, (0,), "sib")
-    got("m_zs")
-    prefix_plane(main, 0, 0)
+    got("m_ps", "m_pzs", "c_ps")
+    plane(3)
+
+    got("c_pp")
+    send("c_pps", cont, 2, (0, 0), "sib")
+    got("c_mm")
+    send("c_mms", cont, 2, (0, 1), "sib")
+    got("m_ppz", "m_mmz")
+    send("m_zzs", main, 2, (0, 1), "sib")
+    got("m_ms", "m_mzs", "c_ms")
+    plane(1)
 
     got("o_p")
     send("o_pp", over, 3, (0, 0), "xp")
@@ -273,19 +296,7 @@
     got("o_m")
     send("o_mm", over, 1, (0, 1), "xm")
     send("o_ms", over, 1, (0,), "sib")
-    got("c_pp")
-    send("c_pps", cont, 2, (0, 0), "sib")
-    got("c_mm")
-    send("c_mms", cont, 2, (0, 1), "sib")
-    got("m_ppz", "m_mmz")
-    send("m_zzs", main, 2, (0, 1), "sib")
-
-    got("m_ps", "m_pzs")
-    prefix_plane(main, 3, 0)
-    got("m_ms", "m_mzs")
-    prefix_plane(main, 1, 0)
-
-    got("c_ps", "c_ms", "c_pps", "c_mms")
+    got("c_pps", "c_mms")
 
     def write_slot(tenant):
         def step(b, carry):
@@ -296,6 +307,7 @@
 
         return lax.fori_loop(0, 16, step, (jnp.int32(0), jnp.int32(0)), unroll=4)
 
+    locals_["wslots"].wait()
     block, slot_0 = write_slot(r)
     i, j = (block + c) % 2, (block // 2 + zl) % 2
     away = (block // 4 + 4 - x) % 4
@@ -306,11 +318,8 @@
     send_to("w_p", wmine, wblk.at[2], "rp")
     send_to("w_m", wmine, wblk.at[0], "rm")
 
-    for k in range(1, 4):
-        pl.when(x + k >= 4)(functools.partial(suffix_plane, k, None))
-    got("o_s")
-    prefix_plane(over, 0, 2)
-
+    got("m_pps", "m_mms", "m_zzs")
+    plane(2)
     got("o_pp")
     send("o_pps", over, 2, (0, 0), "sib")
     got("o_mm")
@@ -319,15 +328,14 @@
     send_to("w_pp", wblk.at[2, 0], wblk.at[1, 0], "rp")
     got("w_m")
     send_to("w_mm", wblk.at[0, 1], wblk.at[1, 1], "rm")
-
-    got("m_pps", "m_mms", "m_zzs")
-    prefix_plane(main, 2, 0)
+    got("o_s")
+    over_plane(0)
     got("o_ps")
-    prefix_plane(over, 3, 2)
+    over_plane(3)
     got("o_ms")
-    prefix_plane(over, 1, 2)
+    over_plane(1)
     got("o_pps", "o_mms")
-    prefix_plane(over, 2, 2)
+    over_plane(2)
 
     slot_1 = write_slot((r + 1) % 4)[1]
     slot_2 = write_slot((r + 2) % 4)[1]
@@ -346,6 +354,7 @@
     lax.fori_loop(0, 20, one_slot, 0)
 
     token = p * 128 + lax.broadcasted_iota(jnp.int32, (128, 128), 0)
+    locals_["slens"].wait()
     live = token < slens[r]
     for h in range(8):
         rows = slice(h * 128, (h + 1) * 128)
@@ -359,8 +368,7 @@
 def local(hidden, base, suffix, pool, down, up, table, plens, slens, adapters, wslots):
     bf, f32 = jnp.bfloat16, jnp.float32
     down = down.transpose(0, 2, 1)
-    smem = pl.BlockSpec(memory_space=pltpu.SMEM)
-    anywhere = pl.BlockSpec(memory_space=pl.ANY)
+    hbm = pl.BlockSpec(memory_space=pltpu.HBM)
     vmem = pl.BlockSpec(memory_space=pltpu.VMEM)
     block = (2, 128, 128)
     return pl.pallas_call(
@@ -369,9 +377,10 @@
             jax.ShapeDtypeStruct(base.shape, bf),
             jax.ShapeDtypeStruct(pool.shape, bf),
         ),
-        in_specs=[smem] * 5 + [anywhere] * 6,
+        in_specs=[hbm] * 11,
         out_specs=(vmem, vmem),
         scratch_shapes=[
+            *[pltpu.SMEM(a.shape, jnp.int32) for a in (table, plens, slens, adapters, wslots)],
             pltpu.VMEM(pool.shape, bf),
             pltpu.VMEM(hidden.shape[1:], bf),
             pltpu.VMEM(base.shape[1:], bf),
@@ -382,20 +391,20 @@
             pltpu.VMEM(block, bf),
             pltpu.VMEM((3,) + block, bf),
             pltpu.VMEM(block, bf),
-            pltpu.VMEM((3, 16, 128), f32),
-            pltpu.VMEM((3, 16, 128), f32),
+            pltpu.VMEM((16, 128), f32),
+            pltpu.VMEM((8, 16, 128), f32),
             pltpu.VMEM((1024, 128), bf),
             pltpu.VMEM((1024, 128), f32),
             pltpu.VMEM((1024, 256), f32),
-            pltpu.VMEM((512, 128), bf),
-            pltpu.VMEM((512, 256), bf),
+            pltpu.VMEM((1536, 128), bf),
+            pltpu.VMEM((1536, 256), bf),
             pltpu.SMEM((64,), jnp.int32),
-            pltpu.SemaphoreType.DMA((6,)),
+            pltpu.SemaphoreType.DMA((11,)),
             pltpu.SemaphoreType.DMA((COPIES,)),
             pltpu.SemaphoreType.DMA((COPIES,)),
         ],
         compiler_params=pltpu.CompilerParams(
-            collective_id=0, has_side_effects=True, vmem_limit_bytes=48 << 20
+            collective_id=0, has_side_effects=True, vmem_limit_bytes=62 << 20
         ),
         name="attend_all",
     )(table, plens, slens, adapters, wslots, hidden, base, suffix, pool, down, up)

time: 70.9 us -> 59.6 us (0.84)
  local copies, waits for them, and re-layouts: 11 us -> 4.19 us
  Pallas kernels: 58.8 us -> 54.6 us
    unnamed x24 -> x2, local copies, waits for them, and re-layouts: 11 us -> 4.19 us
    pallas_call x1, Pallas kernels: 58.8 us -> 54.6 us  [local(): pl.pallas_call(kernel, out_shape=(jax.ShapeDtypeStruct(base.shape, bf), j...]
where the time goes in v2:
time: 59.6 us; the launch traced here: 59.4 us
  Pallas kernels  54.6 us (92%)
  local copies, waits for them, and re-layouts  4.19 us (7%)
  between operations  0.64 us (1%)
    pallas_call x1, Pallas kernels, local(): pl.pallas_call(kernel, out_shape=(jax.ShapeDtypeStruct(base.shape, bf), j...  54.6 us
    unnamed x2, local copies, waits for them, and re-layouts  4.19 us

profile of v2, /device:TPU:64, one launch (start us, length us, event | category | flops | bytes accessed | tf_op | source)
XLA Modules:
  0.0 59.4 jit_solution(5046963350167559013)
XLA Ops:
  0.6 54.6 %attend_all.1 = (bf16[1,128,1024]{2,1,0:T(8,128)(2,1)}, bf16[20,2,128,128]{3,2,1,0:T(8,128)(2,1)}) custom-call(s32[4,32]{1,0:T(4,128)} %table_in.1, s32[4]{0:T(128)} %plens_in.1, s32[4]{0:T(128)} %slens_in.1, s32[4]{0:T(128)} %adapters_in.1, s32[4,16]{1,0:T(4,128)} %wslots_in.1, bf16[1,128,1024]{2,1,0:T(8,128)(2,1)} %hidden.1, bf16[1,128,1024]{2,1,0:T(8,128)(2,1)} %base.1, ...), custom_call_target="tpu_custom_call" | custom-call | tf_op jit(solution)/shard_map/attend_all/pallas_call | solution.py:374
  55.2 1.7 %copy.15 = bf16[1,128,1024]{2,1,0:T(8,128)(2,1)} copy(bf16[1,128,1024]{2,1,0:T(8,128)(2,1)} %get-tuple-element.4) | data formatting | bytes 524288
  56.9 2.5 %copy.16 = bf16[20,2,128,128]{3,2,1,0:T(8,128)(2,1)} copy(bf16[20,2,128,128]{3,2,1,0:T(8,128)(2,1)} %get-tuple-element.5) | data formatting | bytes 2621440

commit v3 on v2

--- a/solution.py
+++ b/solution.py
@@ -13,37 +13,35 @@
 LOG2E = 1.4426950408889634
 LOW = -1e30
 ROWS = 128
-PARTNERS = ("sib", "xp", "xm", "zp", "zn", "y1", "y2", "y3", "y4", "y5", "y6", "y7", "rp", "rm")
-COPIES = 50
+NEAR = ("sib", "xp", "xm", "zp")
+ALONG_TP = (0, 1, 7, 2, 6, 3, 5, 4)
+COPIES = 38
 
 
 def kernel(
     table_in, plens_in, slens_in, adapters_in, wslots_in,
     hidden, base, suffix, pool, down, up,
-    out, pool_out,
+    out, writes,
     table, plens, slens, adapters, wslots,
     pool_v, hid_v, base_v, down_v, up_v,
     main_0, main_1, main_2, main_3, over_0, over_1, over_2, over_3, cont_0, cont_1, cont_2, cont_3,
-    fore, wblk, wmine,
+    wblk, wmine,
     rank_out, rank_in, qs, peak, acc, kc, vc, nval,
-    local_sem, send_sem, recv_sem,
+    local_sem, send_sem, recv_sem, rank_ssem, rank_rsem, write_ssem, write_rsem, here_tp, here_req,
 ):
     p = lax.axis_index("pool")
     y = lax.axis_index("tp")
     r = lax.axis_index("req")
     x, zl, c = p // 4, (p // 2) % 2, p % 2
     x1, x3 = (x + 1) % 4, (x + 3) % 4
-    rn = (r + 2 * zl + 3) % 4
-    other = p + 2 - 4 * zl
+    q = jnp.where(y == 0, 0, jnp.where(y <= 4, 2 * y - 1, 16 - 2 * y))
     partner = {
         "sib": {"pool": p + 1 - 2 * c},
         "xp": {"pool": x1 * 4 + zl * 2 + c},
         "xm": {"pool": x3 * 4 + zl * 2 + c},
-        "zp": {"pool": other},
-        "zn": {"pool": other, "req": rn},
-        **{f"y{d}": {"tp": (y + d) % 8} for d in range(1, 8)},
-        "rp": {"req": (r + 1) % 4},
-        "rm": {"req": (r + 3) % 4},
+        "zp": {"pool": p + 2 - 4 * zl},
+        **{f"y{e}": {"tp": ALONG_TP[e]} for e in range(8)},
+        **{f"r{e}": {"req": e} for e in range(4)},
     }
 
     main = (main_0, main_1, main_2, main_3)
@@ -71,9 +69,21 @@
         locals_[name].start()
 
     barrier = pltpu.get_barrier_semaphore()
-    for name in PARTNERS:
-        pl.semaphore_signal(barrier, inc=1, device_id=partner[name], device_id_type=MESH)
-    pl.semaphore_wait(barrier, len(PARTNERS))
+
+    def signal(sem, to):
+        pl.semaphore_signal(sem, inc=1, device_id=partner[to], device_id_type=MESH)
+
+    for name in NEAR:
+        signal(barrier, name)
+    for e in range(1, 8):
+        pl.when(e > q)(functools.partial(signal, barrier, f"y{e}"))
+    for e in range(1, 4):
+        pl.when(e > r)(functools.partial(signal, barrier, f"r{e}"))
+    pl.semaphore_wait(barrier, len(NEAR) + q + r)
+    for e in range(7):
+        pl.when(e < q)(functools.partial(signal, here_tp.at[q], f"y{e}"))
+    for e in range(3):
+        pl.when(e < r)(functools.partial(signal, here_req.at[r], f"r{e}"))
 
     copies = {}
 
@@ -87,12 +97,36 @@
         copies[name] = copy
         copy.start()
 
+    def spread(mine, src, place, sems, names):
+        there = [
+            pltpu.make_async_remote_copy(
+                src_ref=src, dst_ref=place.at[mine],
+                send_sem=sems[0].at[e], recv_sem=sems[1].at[mine],
+                device_id=partner[name], device_id_type=MESH,
+            )
+            for e, name in enumerate(names)
+        ]
+        here = [
+            pltpu.make_async_remote_copy(
+                src_ref=src, dst_ref=place.at[e],
+                send_sem=sems[0].at[e], recv_sem=sems[1].at[e],
+                device_id=partner[name], device_id_type=MESH,
+            )
+            for e, name in enumerate(names)
+        ]
+
+        def each(what, copies_):
+            for e in range(len(names)):
+                pl.when(e != mine)(getattr(copies_[e], what))
+
+        return functools.partial(each, "start", there), functools.partial(each, "wait_recv", here), functools.partial(each, "wait_send", there)
+
     def send(name, buf, k, at, to):
         there = (k + {"xp": 3, "xm": 1}.get(to, 0)) % 4
         place = list(at)
         if to == "sib":
             place[0] = 1 - at[0]
-        if to in ("zp", "zn"):
+        if to == "zp":
             place[1] = 1 - at[1]
         send_to(name, buf[k].at[at], buf[there].at[tuple(place)], to)
 
@@ -129,19 +163,20 @@
     locals_["down"].wait()
     locals_["adapters"].wait()
     adapter = adapters[r]
-    rank_out[...] = lax.dot_general(
+    part = lax.dot_general(
         down_v[adapter], hid_v[...], (((1,), (1,)), ((), ())), preferred_element_type=jnp.float32
     )
-    for d in range(1, 8):
-        send_to(f"r_{d}", rank_out, rank_in.at[8 - d], f"y{d}")
-
-    theirs = own_slots(rn)
+    rank_out[...] = part
     for k in range(2):
         over_0[0, 0, k] = pool_v[mine[2 + k]]
-    fore[...] = pool_v[theirs[3]]
-    send("o_z", over, 0, (0, 0, 0), "zp")
-    send_to("o_n", fore, over_0.at[0, 1, 1], "zn")
+    send("o_z", over, 0, (0, 0), "zp")
     send("m_s", main, 0, (0, 0), "sib")
+    for e in range(1, 8):
+        pl.when(e > q)(functools.partial(pl.semaphore_wait, here_tp.at[e], 1))
+    rank_send, rank_got, rank_sent = spread(
+        q, rank_out, rank_in, (rank_ssem, rank_rsem), [f"y{e}" for e in range(8)]
+    )
+    rank_send()
 
     got("c_z")
     send("c_p", cont, 0, (0,), "xp")
@@ -170,7 +205,7 @@
 
     lax.fori_loop(0, 16, one_device, 0)
 
-    got("o_z", "o_n")
+    got("o_z")
     send("o_p", over, 0, (0,), "xp")
     send("o_m", over, 0, (0,), "xm")
     send("o_s", over, 0, (0,), "sib")
@@ -182,10 +217,10 @@
     send("m_mm", main, 1, (0, 0, 1), "xm")
     send("m_mz", main, 1, (0, 0), "zp")
     send("m_ms", main, 1, (0, 0), "sib")
-    got(*(f"r_{d}" for d in range(1, 8)))
-    total = rank_out[...]
-    for d in range(1, 8):
-        total = total + rank_in[d]
+    rank_got()
+    total = jnp.zeros(rank_out.shape, jnp.float32)
+    for e in range(8):
+        total = total + jnp.where(e == q, part, rank_in[e])
     rank = total.T.astype(jnp.bfloat16)
     locals_["base"].wait()
     locals_["up"].wait()
@@ -298,25 +333,25 @@
     send("o_ms", over, 1, (0,), "sib")
     got("c_pps", "c_mms")
 
-    def write_slot(tenant):
-        def step(b, carry):
-            block, slot = carry
-            local = wslots[tenant, b] - p * 20
-            owned = (local >= 0) & (local < 20)
-            return jnp.where(owned, b, block), jnp.where(owned, local, slot)
-
-        return lax.fori_loop(0, 16, step, (jnp.int32(0), jnp.int32(0)), unroll=4)
-
     locals_["wslots"].wait()
-    block, slot_0 = write_slot(r)
+
+    def write_step(b, block):
+        local = wslots[r, b] - p * 20
+        return jnp.where((local >= 0) & (local < 20), b, block)
+
+    block = lax.fori_loop(0, 16, write_step, jnp.int32(0), unroll=4)
     i, j = (block + c) % 2, (block // 2 + zl) % 2
     away = (block // 4 + 4 - x) % 4
     chosen = cont_0[i, j]
     for k in range(1, 4):
         chosen = jnp.where(away == k, cont[k][i, j], chosen)
     wmine[...] = chosen
-    send_to("w_p", wmine, wblk.at[2], "rp")
-    send_to("w_m", wmine, wblk.at[0], "rm")
+    for e in range(1, 4):
+        pl.when(e > r)(functools.partial(pl.semaphore_wait, here_req.at[e], 1))
+    write_send, write_got, write_sent = spread(
+        r, wmine, wblk, (write_ssem, write_rsem), [f"r{e}" for e in range(4)]
+    )
+    write_send()
 
     got("m_pps", "m_mms", "m_zzs")
     plane(2)
@@ -324,10 +359,6 @@
     send("o_pps", over, 2, (0, 0), "sib")
     got("o_mm")
     send("o_mms", over, 2, (0, 1), "sib")
-    got("w_p")
-    send_to("w_pp", wblk.at[2, 0], wblk.at[1, 0], "rp")
-    got("w_m")
-    send_to("w_mm", wblk.at[0, 1], wblk.at[1, 1], "rm")
     got("o_s")
     over_plane(0)
     got("o_ps")
@@ -337,21 +368,9 @@
     got("o_pps", "o_mms")
     over_plane(2)
 
-    slot_1 = write_slot((r + 1) % 4)[1]
-    slot_2 = write_slot((r + 2) % 4)[1]
-    slot_3 = write_slot((r + 3) % 4)[1]
-    got("w_pp", "w_mm")
-
-    def one_slot(s, unused):
-        block = pool_v[s]
-        block = jnp.where(s == slot_0, wmine[...], block)
-        block = jnp.where(s == slot_1, wblk[0], block)
-        block = jnp.where(s == slot_2, wblk[1], block)
-        block = jnp.where(s == slot_3, wblk[2], block)
-        pool_out[s] = block
-        return unused
-
-    lax.fori_loop(0, 20, one_slot, 0)
+    write_got()
+    for e in range(4):
+        writes[e] = jnp.where(e == r, wmine[...], wblk[e])
 
     token = p * 128 + lax.broadcasted_iota(jnp.int32, (128, 128), 0)
     locals_["slens"].wait()
@@ -363,6 +382,34 @@
 
     for copy in copies.values():
         copy.wait_send()
+    rank_sent()
+    write_sent()
+
+
+def place(wslots, attended_in, writes, pool, attended, pool_after, sems):
+    p = lax.axis_index("pool")
+    hand_on = pltpu.make_async_copy(attended_in, attended, sems.at[20])
+    hand_on.start()
+
+    def find(tenant):
+        def step(b, slot):
+            local = wslots[tenant, b] - p * 20
+            return jnp.where((local >= 0) & (local < 20), local, slot)
+
+        return lax.fori_loop(0, 16, step, jnp.int32(0), unroll=4)
+
+    slots = [find(tenant) for tenant in range(4)]
+    for s in range(20):
+        kept = True
+        for tenant, slot in enumerate(slots):
+            kept = kept & (slot != s)
+            pl.when(slot == s)(
+                pltpu.make_async_copy(writes.at[tenant], pool_after.at[s], sems.at[s]).start
+            )
+        pl.when(kept)(pltpu.make_async_copy(pool.at[s], pool_after.at[s], sems.at[s]).start)
+    for s in range(20):
+        pltpu.make_async_copy(pool.at[s], pool_after.at[s], sems.at[s]).wait()
+    hand_on.wait()
 
 
 def local(hidden, base, suffix, pool, down, up, table, plens, slens, adapters, wslots):
@@ -371,11 +418,11 @@
     hbm = pl.BlockSpec(memory_space=pltpu.HBM)
     vmem = pl.BlockSpec(memory_space=pltpu.VMEM)
     block = (2, 128, 128)
-    return pl.pallas_call(
+    attended, writes = pl.pallas_call(
         kernel,
         out_shape=(
             jax.ShapeDtypeStruct(base.shape, bf),
-            jax.ShapeDtypeStruct(pool.shape, bf),
+            jax.ShapeDtypeStruct((4,) + block, bf),
         ),
         in_specs=[hbm] * 11,
         out_specs=(vmem, vmem),
@@ -388,8 +435,7 @@
             pltpu.VMEM(up.shape, bf),
             *[pltpu.VMEM((2, 2, 2) + block, bf)] * 8,
             *[pltpu.VMEM((2, 2) + block, bf)] * 4,
-            pltpu.VMEM(block, bf),
-            pltpu.VMEM((3,) + block, bf),
+            pltpu.VMEM((4,) + block, bf),
             pltpu.VMEM(block, bf),
             pltpu.VMEM((16, 128), f32),
             pltpu.VMEM((8, 16, 128), f32),
@@ -402,12 +448,30 @@
             pltpu.SemaphoreType.DMA((11,)),
             pltpu.SemaphoreType.DMA((COPIES,)),
             pltpu.SemaphoreType.DMA((COPIES,)),
+            pltpu.SemaphoreType.DMA((8,)),
+            pltpu.SemaphoreType.DMA((8,)),
+            pltpu.SemaphoreType.DMA((4,)),
+            pltpu.SemaphoreType.DMA((4,)),
+            pltpu.SemaphoreType.REGULAR((8,)),
+            pltpu.SemaphoreType.REGULAR((4,)),
         ],
         compiler_params=pltpu.CompilerParams(
             collective_id=0, has_side_effects=True, vmem_limit_bytes=62 << 20
         ),
         name="attend_all",
     )(table, plens, slens, adapters, wslots, hidden, base, suffix, pool, down, up)
+    return pl.pallas_call(
+        place,
+        out_shape=(
+            jax.ShapeDtypeStruct(base.shape, bf),
+            jax.ShapeDtypeStruct(pool.shape, bf),
+        ),
+        in_specs=[pl.BlockSpec(memory_space=pltpu.SMEM)] + [hbm] * 3,
+        out_specs=(hbm, hbm),
+        scratch_shapes=[pltpu.SemaphoreType.DMA((21,))],
+        compiler_params=pltpu.CompilerParams(vmem_limit_bytes=62 << 20),
+        name="place",
+    )(wslots, attended, writes, pool)
 
 
 def solution(mesh):

time: 59.6 us -> 95.8 us (1.61)
  the two profiles are of different devices: /device:TPU:64 before, /device:TPU:384 now
where the time goes in v3:
time: 95.8 us; the launch traced here: 95.7 us
  Pallas kernels  94.8 us (99%)
    pallas_call x1, Pallas kernels, local(): pl.pallas_call(place, out_shape=(jax.ShapeDtypeStruct(base.shape, bf), ja...  49.6 us
    pallas_call x1, Pallas kernels, local(): pl.pallas_call(kernel, out_shape=(jax.ShapeDtypeStruct(base.shape, bf), j...  45.2 us

profile of v3, /device:TPU:384, one launch (start us, length us, event | category | flops | bytes accessed | tf_op | source)
XLA Modules:
  0.0 95.7 jit_solution(17814887514273162337)
XLA Ops:
  0.6 45.2 %attend_all.1 = (bf16[1,128,1024]{2,1,0:T(8,128)(2,1)}, bf16[4,2,128,128]{3,2,1,0:T(8,128)(2,1)}) custom-call(s32[4,32]{1,0:T(4,128)} %table_in.1, s32[4]{0:T(128)} %plens_in.1, s32[4]{0:T(128)} %slens_in.1, s32[4]{0:T(128)} %adapters_in.1, s32[4,16]{1,0:T(4,128)} %wslots.1, bf16[1,128,1024]{2,1,0:T(8,128)(2,1)} %hidden.1, bf16[1,128,1024]{2,1,0:T(8,128)(2,1)} %base.1, ...), custom_call_target="tpu_custom_call" | custom-call | tf_op jit(solution)/shard_map/attend_all/pallas_call | solution.py:421
  45.9 49.6 %place.1 = (bf16[1,128,1024]{2,1,0:T(8,128)(2,1)}, bf16[20,2,128,128]{3,2,1,0:T(8,128)(2,1)}) custom-call(s32[4,16]{1,0:T(4,128)} %wslots.1, bf16[1,128,1024]{2,1,0:T(8,128)(2,1)} %get-tuple-element.4.attended_in, bf16[4,2,128,128]{3,2,1,0:T(8,128)(2,1)} %get-tuple-element.5.writes, bf16[20,2,128,128]{3,2,1,0:T(8,128)(2,1)} %pool.3), custom_call_target="tpu_custom_call" | custom-call | tf_op jit(solution)/shard_map/place/pallas_call | solution.py:463

commit v4 on v3

--- a/solution.py
+++ b/solution.py
@@ -26,7 +26,7 @@
     pool_v, hid_v, base_v, down_v, up_v,
     main_0, main_1, main_2, main_3, over_0, over_1, over_2, over_3, cont_0, cont_1, cont_2, cont_3,
     wblk, wmine,
-    rank_out, rank_in, qs, peak, acc, kc, vc, nval,
+    rank_out, rank_in, qs, peak, acc, kc, vc, lines, nval,
     local_sem, send_sem, recv_sem, rank_ssem, rank_rsem, write_ssem, write_rsem, here_tp, here_req,
 ):
     p = lax.axis_index("pool")
@@ -62,6 +62,7 @@
         ("base", base.at[0], base_v),
         ("up", up, up_v),
         ("plens", plens_in, plens),
+        ("lines", table_in, lines),
         ("slens", slens_in, slens),
         ("wslots", wslots_in, wslots),
     )):
@@ -157,7 +158,9 @@
         main_0[0, 0, k] = pool_v[mine[k]]
     send("m_p", main, 0, (0, 0), "xp")
     send("m_m", main, 0, (0, 0), "xm")
-    send("m_z", main, 0, (0, 0), "zp")
+    for k in range(2):
+        over_0[0, 0, k] = pool_v[mine[2 + k]]
+    send("o_z", over, 0, (0, 0), "zp")
 
     locals_["hidden"].wait()
     locals_["down"].wait()
@@ -167,9 +170,12 @@
         down_v[adapter], hid_v[...], (((1,), (1,)), ((), ())), preferred_element_type=jnp.float32
     )
     rank_out[...] = part
-    for k in range(2):
-        over_0[0, 0, k] = pool_v[mine[2 + k]]
-    send("o_z", over, 0, (0, 0), "zp")
+
+    got("c_z")
+    send("c_p", cont, 0, (0,), "xp")
+    send("c_m", cont, 0, (0,), "xm")
+    send("c_s", cont, 0, (0,), "sib")
+    send("m_z", main, 0, (0, 0), "zp")
     send("m_s", main, 0, (0, 0), "sib")
     for e in range(1, 8):
         pl.when(e > q)(functools.partial(pl.semaphore_wait, here_tp.at[e], 1))
@@ -178,37 +184,20 @@
     )
     rank_send()
 
-    got("c_z")
-    send("c_p", cont, 0, (0,), "xp")
-    send("c_m", cont, 0, (0,), "xm")
-    send("c_s", cont, 0, (0,), "sib")
-
     locals_["plens"].wait()
-    plen = plens[r]
-
-    def one_device(d, unused):
-        def step(b, carry):
-            count, rows = carry
-            local = table[r, b] - d * 20
-            owned = (local >= 0) & (local < 20)
-            seen = plen - b * 128
-            rows = tuple(
-                jnp.where(owned & (count == k), seen, row) for k, row in enumerate(rows)
-            )
-            return count + owned.astype(jnp.int32), rows
-
-        zero = jnp.int32(0)
-        rows = lax.fori_loop(0, 32, step, (zero, (zero,) * 4), unroll=4)[1]
-        for k in range(4):
-            nval[d * 4 + k] = rows[k]
-        return unused
-
-    lax.fori_loop(0, 16, one_device, 0)
-
-    got("o_z")
-    send("o_p", over, 0, (0,), "xp")
-    send("o_m", over, 0, (0,), "xm")
-    send("o_s", over, 0, (0,), "sib")
+    locals_["lines"].wait()
+    device = lax.broadcasted_iota(jnp.int32, (16, 32), 0) * 20
+    line = lines[pl.ds(r, 1), :]
+    owned = ((line >= device) & (line < device + 20)).astype(jnp.float32)
+    before = lax.broadcasted_iota(jnp.int32, (32, 32), 0) < lax.broadcasted_iota(jnp.int32, (32, 32), 1)
+    order = jnp.dot(
+        owned.astype(jnp.bfloat16), before.astype(jnp.bfloat16), preferred_element_type=jnp.float32
+    )
+    rest = (plens[r] - lax.broadcasted_iota(jnp.int32, (16, 32), 1) * 128).astype(jnp.float32)
+    for k in range(4):
+        rows = jnp.sum(jnp.where(order == k, owned * rest, 0.0), axis=1, keepdims=True)
+        nval[k] = jnp.broadcast_to(rows, (16, 128))
+
     got("m_p")
     send("m_pp", main, 3, (0, 0, 0), "xp")
     send("m_pz", main, 3, (0, 0), "zp")
@@ -234,7 +223,7 @@
     scale = HD**-0.5 * LOG2E
     own_key = cont_0[0, 0, 0, 0:1, :]
 
-    row_no = lax.broadcasted_iota(jnp.int32, (128, 128), 0)
+    row_no = lax.broadcasted_iota(jnp.int32, (128, 128), 0).astype(jnp.float32)
 
     def fill(n, block, rows):
         at = slice(n * 128, (n + 1) * 128)
@@ -274,12 +263,12 @@
     def slots(buf, k, first):
         for n in range(8):
             i, j, slot = n // 4, n // 2 % 2, n % 2
-            fill(n, buf[k][i, j, slot], nval[device_of(k, i, j) * 4 + first + slot])
+            fill(n, buf[k][i, j, slot], nval[first + slot, pl.ds(device_of(k, i, j), 1), :])
 
     def plane(k):
         slots(main, k, 0)
         for n in range(4):
-            fill(8 + n, cont[k][n // 2, n % 2], 128 if k == 0 else jnp.where(x + k >= 4, 128, 0))
+            fill(8 + n, cont[k][n // 2, n % 2], 128.0 if k == 0 else jnp.where(x + k >= 4, 128.0, 0.0))
         mask = None
         if k == 0:
             lane = lax.broadcasted_iota(jnp.int32, (ROWS, 128), 1)
@@ -293,17 +282,26 @@
         slots(over, k, 2)
         attend(1024)
 
-    got("m_z", "m_s")
-    send("m_zs", main, 0, (0, 1), "sib")
-    got("c_s", "m_zs")
-    plane(0)
-
     got("c_p")
     send("c_pp", cont, 3, (0, 0), "xp")
     send("c_ps", cont, 3, (0,), "sib")
     got("c_m")
     send("c_mm", cont, 1, (0, 1), "xm")
     send("c_ms", cont, 1, (0,), "sib")
+    got("o_z")
+    send("o_p", over, 0, (0,), "xp")
+    send("o_m", over, 0, (0,), "xm")
+    send("o_s", over, 0, (0,), "sib")
+
+    got("m_z", "m_s")
+    send("m_zs", main, 0, (0, 1), "sib")
+    got("c_s", "m_zs")
+    plane(0)
+
+    got("c_pp")
+    send("c_pps", cont, 2, (0, 0), "sib")
+    got("c_mm")
+    send("c_mms", cont, 2, (0, 1), "sib")
     got("m_pz", "m_mz")
     send("m_pzs", main, 3, (0, 1), "sib")
     send("m_mzs", main, 1, (0, 1), "sib")
@@ -316,22 +314,7 @@
     got("m_ps", "m_pzs", "c_ps")
     plane(3)
 
-    got("c_pp")
-    send("c_pps", cont, 2, (0, 0), "sib")
-    got("c_mm")
-    send("c_mms", cont, 2, (0, 1), "sib")
-    got("m_ppz", "m_mmz")
-    send("m_zzs", main, 2, (0, 1), "sib")
-    got("m_ms", "m_mzs", "c_ms")
-    plane(1)
-
-    got("o_p")
-    send("o_pp", over, 3, (0, 0), "xp")
-    send("o_ps", over, 3, (0,), "sib")
-    got("o_m")
-    send("o_mm", over, 1, (0, 1), "xm")
-    send("o_ms", over, 1, (0,), "sib")
-    got("c_pps", "c_mms")
+    got("c_ms", "c_pps", "c_mms")
 
     locals_["wslots"].wait()
 
@@ -352,6 +335,17 @@
         r, wmine, wblk, (write_ssem, write_rsem), [f"r{e}" for e in range(4)]
     )
     write_send()
+
+    got("o_p")
+    send("o_pp", over, 3, (0, 0), "xp")
+    send("o_ps", over, 3, (0,), "sib")
+    got("o_m")
+    send("o_mm", over, 1, (0, 1), "xm")
+    send("o_ms", over, 1, (0,), "sib")
+    got("m_ppz", "m_mmz")
+    send("m_zzs", main, 2, (0, 1), "sib")
+    got("m_ms", "m_mzs")
+    plane(1)
 
     got("m_pps", "m_mms", "m_zzs")
     plane(2)
@@ -386,10 +380,11 @@
     write_sent()
 
 
-def place(wslots, attended_in, writes, pool, attended, pool_after, sems):
+def place(wslots, attended_in, writes, pool, attended, pool_after, held, blocks, in_sem, out_sem):
     p = lax.axis_index("pool")
-    hand_on = pltpu.make_async_copy(attended_in, attended, sems.at[20])
-    hand_on.start()
+    first = pltpu.make_async_copy(attended_in, held, in_sem.at[20])
+    second = pltpu.make_async_copy(held, attended, out_sem.at[20])
+    first.start()
 
     def find(tenant):
         def step(b, slot):
@@ -404,12 +399,17 @@
         for tenant, slot in enumerate(slots):
             kept = kept & (slot != s)
             pl.when(slot == s)(
-                pltpu.make_async_copy(writes.at[tenant], pool_after.at[s], sems.at[s]).start
-            )
-        pl.when(kept)(pltpu.make_async_copy(pool.at[s], pool_after.at[s], sems.at[s]).start)
+                pltpu.make_async_copy(writes.at[tenant], blocks.at[s], in_sem.at[s]).start
+            )
+        pl.when(kept)(pltpu.make_async_copy(pool.at[s], blocks.at[s], in_sem.at[s]).start)
+    first.wait()
+    second.start()
     for s in range(20):
-        pltpu.make_async_copy(pool.at[s], pool_after.at[s], sems.at[s]).wait()
-    hand_on.wait()
+        pltpu.make_async_copy(pool.at[s], blocks.at[s], in_sem.at[s]).wait()
+        pltpu.make_async_copy(blocks.at[s], pool_after.at[s], out_sem.at[s]).start()
+    for s in range(20):
+        pltpu.make_async_copy(blocks.at[s], pool_after.at[s], out_sem.at[s]).wait()
+    second.wait()
 
 
 def local(hidden, base, suffix, pool, down, up, table, plens, slens, adapters, wslots):
@@ -444,8 +444,9 @@
             pltpu.VMEM((1024, 256), f32),
             pltpu.VMEM((1536, 128), bf),
             pltpu.VMEM((1536, 256), bf),
-            pltpu.SMEM((64,), jnp.int32),
-            pltpu.SemaphoreType.DMA((11,)),
+            pltpu.VMEM(table.shape, jnp.int32),
+            pltpu.VMEM((4, 16, 128), f32),
+            pltpu.SemaphoreType.DMA((12,)),
             pltpu.SemaphoreType.DMA((COPIES,)),
             pltpu.SemaphoreType.DMA((COPIES,)),
             pltpu.SemaphoreType.DMA((8,)),
@@ -468,7 +469,12 @@
         ),
         in_specs=[pl.BlockSpec(memory_space=pltpu.SMEM)] + [hbm] * 3,
         out_specs=(hbm, hbm),
-        scratch_shapes=[pltpu.SemaphoreType.DMA((21,))],
+        scratch_shapes=[
+            pltpu.VMEM(base.shape, bf),
+            pltpu.VMEM(pool.shape, bf),
+            pltpu.SemaphoreType.DMA((21,)),
+            pltpu.SemaphoreType.DMA((21,)),
+        ],
         compiler_params=pltpu.CompilerParams(vmem_limit_bytes=62 << 20),
         name="place",
     )(wslots, attended, writes, pool)

time: 95.8 us -> 46.4 us (0.48)
  the two profiles are of different devices: /device:TPU:384 before, /device:TPU:1 now
where the time goes in v4:
time: 46.4 us; the launch traced here: 46.2 us
  Pallas kernels  45.4 us (98%)
  between operations  0.8 us (2%)
    pallas_call x1, Pallas kernels, local(): pl.pallas_call(kernel, out_shape=(jax.ShapeDtypeStruct(base.shape, bf), j...  42.1 us
    pallas_call x1, Pallas kernels, local(): pl.pallas_call(place, out_shape=(jax.ShapeDtypeStruct(base.shape, bf), ja...  3.29 us

profile of v4, /device:TPU:1, one launch (start us, length us, event | category | flops | bytes accessed | tf_op | source)
XLA Modules:
  0.0 46.2 jit_solution(17236289874182660703)
XLA Ops:
  0.6 42.1 %attend_all.1 = (bf16[1,128,1024]{2,1,0:T(8,128)(2,1)}, bf16[4,2,128,128]{3,2,1,0:T(8,128)(2,1)}) custom-call(s32[4,32]{1,0:T(4,128)} %table_in.1, s32[4]{0:T(128)} %plens_in.1, s32[4]{0:T(128)} %slens_in.1, s32[4]{0:T(128)} %adapters_in.1, s32[4,16]{1,0:T(4,128)} %wslots.1, bf16[1,128,1024]{2,1,0:T(8,128)(2,1)} %hidden.1, bf16[1,128,1024]{2,1,0:T(8,128)(2,1)} %base.1, ...), custom_call_target="tpu_custom_call" | custom-call | tf_op jit(solution)/shard_map/attend_all/pallas_call | solution.py:421
  42.7 3.3 %place.1 = (bf16[1,128,1024]{2,1,0:T(8,128)(2,1)}, bf16[20,2,128,128]{3,2,1,0:T(8,128)(2,1)}) custom-call(s32[4,16]{1,0:T(4,128)} %wslots.1, bf16[1,128,1024]{2,1,0:T(8,128)(2,1)} %get-tuple-element.4.attended_in, bf16[4,2,128,128]{3,2,1,0:T(8,128)(2,1)} %get-tuple-element.5.writes, bf16[20,2,128,128]{3,2,1,0:T(8,128)(2,1)} %pool.3), custom_call_target="tpu_custom_call" | custom-call | tf_op jit(solution)/shard_map/place/pallas_call | solution.py:464

commit v5 on v4

--- a/solution.py
+++ b/solution.py
@@ -24,9 +24,9 @@
     out, writes,
     table, plens, slens, adapters, wslots,
     pool_v, hid_v, base_v, down_v, up_v,
-    main_0, main_1, main_2, main_3, over_0, over_1, over_2, over_3, cont_0, cont_1, cont_2, cont_3,
+    main_0, main_1, main_2, main_3, over_all, cont_0, cont_1, cont_2, cont_3,
     wblk, wmine,
-    rank_out, rank_in, qs, peak, acc, kc, vc, lines, nval,
+    rank_out, rank_in, qs, peak, acc, kc, vc, lines, nval, list_v, listed,
     local_sem, send_sem, recv_sem, rank_ssem, rank_rsem, write_ssem, write_rsem, here_tp, here_req,
 ):
     p = lax.axis_index("pool")
@@ -45,7 +45,7 @@
     }
 
     main = (main_0, main_1, main_2, main_3)
-    over = (over_0, over_1, over_2, over_3)
+    over = [over_all.at[k] for k in range(4)]
     cont = (cont_0, cont_1, cont_2, cont_3)
 
     def device_of(k, i, j):
@@ -159,8 +159,9 @@
     send("m_p", main, 0, (0, 0), "xp")
     send("m_m", main, 0, (0, 0), "xm")
     for k in range(2):
-        over_0[0, 0, k] = pool_v[mine[2 + k]]
+        over_all[0, 0, 0, k] = pool_v[mine[2 + k]]
     send("o_z", over, 0, (0, 0), "zp")
+    send("m_s", main, 0, (0, 0), "sib")
 
     locals_["hidden"].wait()
     locals_["down"].wait()
@@ -176,7 +177,6 @@
     send("c_m", cont, 0, (0,), "xm")
     send("c_s", cont, 0, (0,), "sib")
     send("m_z", main, 0, (0, 0), "zp")
-    send("m_s", main, 0, (0, 0), "sib")
     for e in range(1, 8):
         pl.when(e > q)(functools.partial(pl.semaphore_wait, here_tp.at[e], 1))
     rank_send, rank_got, rank_sent = spread(
@@ -197,6 +197,23 @@
     for k in range(4):
         rows = jnp.sum(jnp.where(order == k, owned * rest, 0.0), axis=1, keepdims=True)
         nval[k] = jnp.broadcast_to(rows, (16, 128))
+    more = jnp.maximum(jnp.sum(owned, axis=1, keepdims=True) - 2.0, 0.0)
+    more = jnp.broadcast_to(more, (16, 128))
+    above = lax.broadcasted_iota(jnp.int32, (16, 16), 1) < lax.broadcasted_iota(jnp.int32, (16, 16), 0)
+    ahead = jnp.dot(
+        above.astype(jnp.bfloat16), more.astype(jnp.bfloat16), preferred_element_type=jnp.float32
+    )
+    lane = lax.broadcasted_iota(jnp.int32, (16, 128), 1).astype(jnp.float32)
+    number = lax.broadcasted_iota(jnp.int32, (16, 128), 0).astype(jnp.float32)
+    third = jnp.where((more > 0.5) & (ahead == lane), 1.0, 0.0)
+    fourth = jnp.where((more > 1.5) & (ahead + 1.0 == lane), 1.0, 0.0)
+    names = jnp.sum(third * (2.0 * number) + fourth * (2.0 * number + 1.0), axis=0, keepdims=True)
+    rows = jnp.sum(third * nval[2] + fourth * nval[3], axis=0, keepdims=True)
+    list_v[...] = jnp.zeros(list_v.shape, jnp.int32)
+    list_v[0:1, :] = names.astype(jnp.int32)
+    list_v[1:2, :] = rows.astype(jnp.int32)
+    list_copy = pltpu.make_async_copy(list_v, listed, local_sem.at[12])
+    list_copy.start()
 
     got("m_p")
     send("m_pp", main, 3, (0, 0, 0), "xp")
@@ -206,6 +223,10 @@
     send("m_mm", main, 1, (0, 0, 1), "xm")
     send("m_mz", main, 1, (0, 0), "zp")
     send("m_ms", main, 1, (0, 0), "sib")
+    got("o_z")
+    send("o_p", over, 0, (0,), "xp")
+    send("o_m", over, 0, (0,), "xm")
+    send("o_s", over, 0, (0,), "sib")
     rank_got()
     total = jnp.zeros(rank_out.shape, jnp.float32)
     for e in range(8):
@@ -232,7 +253,7 @@
         vc[at, :128] = jnp.where(seen, block[1], jnp.bfloat16(0))
         vc[at, 128:] = jnp.where(seen, jnp.bfloat16(1), jnp.bfloat16(0))
 
-    def attend(size, mask=None):
+    def attend(size, mask=None, tiles=range(1024 // ROWS)):
         keys = kc[:size, :]
         values = vc[:size, :]
 
@@ -245,11 +266,11 @@
                 s = jnp.concatenate([s[:, :-512], jnp.where(mask, s[:, -512:], LOW)], axis=1)
             return s
 
-        later = scores(0)
-        for t in range(1024 // ROWS):
+        later = scores(tiles[0])
+        for t in tiles:
             rows = slice(t * ROWS, (t + 1) * ROWS)
             s = later
-            if t + 1 < 1024 // ROWS:
+            if t + 1 in tiles:
                 later = scores(t + 1)
             old = peak[rows, 0:1]
             new = jnp.maximum(old, jnp.max(s, axis=1, keepdims=True))
@@ -260,13 +281,10 @@
             )
             peak[rows, :] = jnp.broadcast_to(new, (ROWS, 128))
 
-    def slots(buf, k, first):
+    def plane(k, between):
         for n in range(8):
             i, j, slot = n // 4, n // 2 % 2, n % 2
-            fill(n, buf[k][i, j, slot], nval[first + slot, pl.ds(device_of(k, i, j), 1), :])
-
-    def plane(k):
-        slots(main, k, 0)
+            fill(n, main[k][i, j, slot], nval[slot, pl.ds(device_of(k, i, j), 1), :])
         for n in range(4):
             fill(8 + n, cont[k][n // 2, n % 2], 128.0 if k == 0 else jnp.where(x + k >= 4, 128.0, 0.0))
         mask = None
@@ -276,11 +294,33 @@
             mask = jnp.concatenate(
                 [lane + device_of(0, n // 2, n % 2) * 128 <= token for n in range(4)], axis=1
             )
-        attend(1536, mask)
-
-    def over_plane(k):
-        slots(over, k, 2)
-        attend(1024)
+        half = 512 // ROWS
+        attend(1536, mask, range(half))
+        between()
+        attend(1536, mask, range(half, 2 * half))
+
+    def start_writes():
+        got("c_ms", "c_pps", "c_mms")
+        locals_["wslots"].wait()
+
+        def write_step(b, block):
+            local = wslots[r, b] - p * 20
+            return jnp.where((local >= 0) & (local < 20), b, block)
+
+        block = lax.fori_loop(0, 16, write_step, jnp.int32(0), unroll=4)
+        i, j = (block + c) % 2, (block // 2 + zl) % 2
+        away = (block // 4 + 4 - x) % 4
+        chosen = cont_0[i, j]
+        for k in range(1, 4):
+            chosen = jnp.where(away == k, cont[k][i, j], chosen)
+        wmine[...] = chosen
+        for e in range(1, 4):
+            pl.when(e > r)(functools.partial(pl.semaphore_wait, here_req.at[e], 1))
+        spread_writes = spread(
+            r, wmine, wblk, (write_ssem, write_rsem), [f"r{e}" for e in range(4)]
+        )
+        spread_writes[0]()
+        return spread_writes
 
     got("c_p")
     send("c_pp", cont, 3, (0, 0), "xp")
@@ -288,15 +328,11 @@
     got("c_m")
     send("c_mm", cont, 1, (0, 1), "xm")
     send("c_ms", cont, 1, (0,), "sib")
-    got("o_z")
-    send("o_p", over, 0, (0,), "xp")
-    send("o_m", over, 0, (0,), "xm")
-    send("o_s", over, 0, (0,), "sib")
 
     got("m_z", "m_s")
     send("m_zs", main, 0, (0, 1), "sib")
     got("c_s", "m_zs")
-    plane(0)
+    plane(0, lambda: None)
 
     got("c_pp")
     send("c_pps", cont, 2, (0, 0), "sib")
@@ -312,29 +348,9 @@
     send("m_mmz", main, 2, (0, 0, 1), "zp")
     send("m_mms", main, 2, (0, 0, 1), "sib")
     got("m_ps", "m_pzs", "c_ps")
-    plane(3)
-
-    got("c_ms", "c_pps", "c_mms")
-
-    locals_["wslots"].wait()
-
-    def write_step(b, block):
-        local = wslots[r, b] - p * 20
-        return jnp.where((local >= 0) & (local < 20), b, block)
-
-    block = lax.fori_loop(0, 16, write_step, jnp.int32(0), unroll=4)
-    i, j = (block + c) % 2, (block // 2 + zl) % 2
-    away = (block // 4 + 4 - x) % 4
-    chosen = cont_0[i, j]
-    for k in range(1, 4):
-        chosen = jnp.where(away == k, cont[k][i, j], chosen)
-    wmine[...] = chosen
-    for e in range(1, 4):
-        pl.when(e > r)(functools.partial(pl.semaphore_wait, here_req.at[e], 1))
-    write_send, write_got, write_sent = spread(
-        r, wmine, wblk, (write_ssem, write_rsem), [f"r{e}" for e in range(4)]
-    )
-    write_send()
+    held = []
+    plane(3, lambda: held.append(start_writes()))
+    write_send, write_got, write_sent = held[0]
 
     got("o_p")
     send("o_pp", over, 3, (0, 0), "xp")
@@ -345,22 +361,24 @@
     got("m_ppz", "m_mmz")
     send("m_zzs", main, 2, (0, 1), "sib")
     got("m_ms", "m_mzs")
-    plane(1)
+    plane(1, lambda: None)
+
+    def last_hop():
+        got("o_pp")
+        send("o_pps", over, 2, (0, 0), "sib")
+        got("o_mm")
+        send("o_mms", over, 2, (0, 1), "sib")
 
     got("m_pps", "m_mms", "m_zzs")
-    plane(2)
-    got("o_pp")
-    send("o_pps", over, 2, (0, 0), "sib")
-    got("o_mm")
-    send("o_mms", over, 2, (0, 1), "sib")
-    got("o_s")
-    over_plane(0)
-    got("o_ps")
-    over_plane(3)
-    got("o_ms")
-    over_plane(1)
-    got("o_pps", "o_mms")
-    over_plane(2)
+    plane(2, last_hop)
+    got("o_s", "o_ps", "o_ms", "o_pps", "o_mms")
+    list_copy.wait()
+    for n in range(16):
+        name = listed[0, n]
+        d = name // 2
+        away, i, j = (d // 4 + 4 - x) % 4, (d + c) % 2, (d // 2 + zl) % 2
+        fill(n, over_all[away, i, j, name % 2], listed[1, n].astype(jnp.float32))
+    attend(2048)
 
     write_got()
     for e in range(4):
@@ -380,11 +398,14 @@
     write_sent()
 
 
-def place(wslots, attended_in, writes, pool, attended, pool_after, held, blocks, in_sem, out_sem):
+def place(wslots, attended_in, writes, pool, attended, pool_after, held, blocks, written, in_sem, out_sem):
     p = lax.axis_index("pool")
-    first = pltpu.make_async_copy(attended_in, held, in_sem.at[20])
-    second = pltpu.make_async_copy(held, attended, out_sem.at[20])
-    first.start()
+    arrivals = [
+        pltpu.make_async_copy(src, dst, in_sem.at[n])
+        for n, (src, dst) in enumerate(((pool, blocks), (attended_in, held), (writes, written)))
+    ]
+    for copy in arrivals:
+        copy.start()
 
     def find(tenant):
         def step(b, slot):
@@ -394,22 +415,17 @@
         return lax.fori_loop(0, 16, step, jnp.int32(0), unroll=4)
 
     slots = [find(tenant) for tenant in range(4)]
-    for s in range(20):
-        kept = True
-        for tenant, slot in enumerate(slots):
-            kept = kept & (slot != s)
-            pl.when(slot == s)(
-                pltpu.make_async_copy(writes.at[tenant], blocks.at[s], in_sem.at[s]).start
-            )
-        pl.when(kept)(pltpu.make_async_copy(pool.at[s], blocks.at[s], in_sem.at[s]).start)
-    first.wait()
+    arrivals[1].wait()
+    second = pltpu.make_async_copy(held, attended, out_sem.at[0])
     second.start()
-    for s in range(20):
-        pltpu.make_async_copy(pool.at[s], blocks.at[s], in_sem.at[s]).wait()
-        pltpu.make_async_copy(blocks.at[s], pool_after.at[s], out_sem.at[s]).start()
-    for s in range(20):
-        pltpu.make_async_copy(blocks.at[s], pool_after.at[s], out_sem.at[s]).wait()
+    arrivals[2].wait()
+    arrivals[0].wait()
+    for tenant, slot in enumerate(slots):
+        blocks[slot] = written[tenant]
+    last = pltpu.make_async_copy(blocks, pool_after, out_sem.at[1])
+    last.start()
     second.wait()
+    last.wait()
 
 
 def local(hidden, base, suffix, pool, down, up, table, plens, slens, adapters, wslots):
@@ -433,7 +449,8 @@
             pltpu.VMEM(base.shape[1:], bf),
             pltpu.VMEM(down.shape, bf),
             pltpu.VMEM(up.shape, bf),
-            *[pltpu.VMEM((2, 2, 2) + block, bf)] * 8,
+            *[pltpu.VMEM((2, 2, 2) + block, bf)] * 4,
+            pltpu.VMEM((4, 2, 2, 2) + block, bf),
             *[pltpu.VMEM((2, 2) + block, bf)] * 4,
             pltpu.VMEM((4,) + block, bf),
             pltpu.VMEM(block, bf),
@@ -442,11 +459,13 @@
             pltpu.VMEM((1024, 128), bf),
             pltpu.VMEM((1024, 128), f32),
             pltpu.VMEM((1024, 256), f32),
-            pltpu.VMEM((1536, 128), bf),
-            pltpu.VMEM((1536, 256), bf),
+            pltpu.VMEM((2048, 128), bf),
+            pltpu.VMEM((2048, 256), bf),
             pltpu.VMEM(table.shape, jnp.int32),
             pltpu.VMEM((4, 16, 128), f32),
-            pltpu.SemaphoreType.DMA((12,)),
+            pltpu.VMEM((8, 128), jnp.int32),
+            pltpu.SMEM((8, 128), jnp.int32),
+            pltpu.SemaphoreType.DMA((13,)),
             pltpu.SemaphoreType.DMA((COPIES,)),
             pltpu.SemaphoreType.DMA((COPIES,)),
             pltpu.SemaphoreType.DMA((8,)),
@@ -472,8 +491,9 @@
         scratch_shapes=[
             pltpu.VMEM(base.shape, bf),
             pltpu.VMEM(pool.shape, bf),
-            pltpu.SemaphoreType.DMA((21,)),
-            pltpu.SemaphoreType.DMA((21,)),
+            pltpu.VMEM(writes.shape, bf),
+            pltpu.SemaphoreType.DMA((3,)),
+            pltpu.SemaphoreType.DMA((2,)),
         ],
         compiler_params=pltpu.CompilerParams(vmem_limit_bytes=62 << 20),
         name="place",

time: 46.4 us -> 45.1 us (0.972)
  Pallas kernels: 45.4 us -> 43.9 us
    pallas_call x1, Pallas kernels: 42.1 us -> 40.7 us  [local(): pl.pallas_call(kernel, out_shape=(jax.ShapeDtypeStruct(base.shape, bf), j...]
where the time goes in v5:
time: 45.1 us; the launch traced here: 44.7 us
  Pallas kernels  43.9 us (97%)
  between operations  0.8 us (2%)
    pallas_call x1, Pallas kernels, local(): pl.pallas_call(kernel, out_shape=(jax.ShapeDtypeStruct(base.shape, bf), j...  40.7 us
    pallas_call x1, Pallas kernels, local(): pl.pallas_call(place, out_shape=(jax.ShapeDtypeStruct(base.shape, bf), ja...  3.23 us

profile of v5, /device:TPU:1, one launch (start us, length us, event | category | flops | bytes accessed | tf_op | source)
XLA Modules:
  0.0 44.7 jit_solution(5933445348413520926)
XLA Ops:
  0.6 40.7 %attend_all.1 = (bf16[1,128,1024]{2,1,0:T(8,128)(2,1)}, bf16[4,2,128,128]{3,2,1,0:T(8,128)(2,1)}) custom-call(s32[4,32]{1,0:T(4,128)} %table_in.1, s32[4]{0:T(128)} %plens_in.1, s32[4]{0:T(128)} %slens_in.1, s32[4]{0:T(128)} %adapters_in.1, s32[4,16]{1,0:T(4,128)} %wslots.1, bf16[1,128,1024]{2,1,0:T(8,128)(2,1)} %hidden.1, bf16[1,128,1024]{2,1,0:T(8,128)(2,1)} %base.1, ...), custom_call_target="tpu_custom_call" | custom-call | tf_op jit(solution)/shard_map/attend_all/pallas_call | solution.py:437
  41.3 3.2 %place.1 = (bf16[1,128,1024]{2,1,0:T(8,128)(2,1)}, bf16[20,2,128,128]{3,2,1,0:T(8,128)(2,1)}) custom-call(s32[4,16]{1,0:T(4,128)} %wslots.1, bf16[1,128,1024]{2,1,0:T(8,128)(2,1)} %get-tuple-element.4.attended_in, bf16[4,2,128,128]{3,2,1,0:T(8,128)(2,1)} %get-tuple-element.5.writes, bf16[20,2,128,128]{3,2,1,0:T(8,128)(2,1)} %pool.3), custom_call_target="tpu_custom_call" | custom-call | tf_op jit(solution)/shard_map/place/pallas_call | solution.py:483

commit v6 on v5

--- a/solution.py
+++ b/solution.py
@@ -332,12 +332,14 @@
     got("m_z", "m_s")
     send("m_zs", main, 0, (0, 1), "sib")
     got("c_s", "m_zs")
-    plane(0, lambda: None)
-
-    got("c_pp")
-    send("c_pps", cont, 2, (0, 0), "sib")
-    got("c_mm")
-    send("c_mms", cont, 2, (0, 1), "sib")
+    def second_hop():
+        got("c_pp")
+        send("c_pps", cont, 2, (0, 0), "sib")
+        got("c_mm")
+        send("c_mms", cont, 2, (0, 1), "sib")
+
+    plane(0, second_hop)
+
     got("m_pz", "m_mz")
     send("m_pzs", main, 3, (0, 1), "sib")
     send("m_mzs", main, 1, (0, 1), "sib")
@@ -348,9 +350,8 @@
     send("m_mmz", main, 2, (0, 0, 1), "zp")
     send("m_mms", main, 2, (0, 0, 1), "sib")
     got("m_ps", "m_pzs", "c_ps")
-    held = []
-    plane(3, lambda: held.append(start_writes()))
-    write_send, write_got, write_sent = held[0]
+    write_send, write_got, write_sent = start_writes()
+    plane(3, lambda: None)
 
     got("o_p")
     send("o_pp", over, 3, (0, 0), "xp")

time: 45.1 us -> 46.5 us (1.031)
  Pallas kernels: 43.9 us -> 45 us
    pallas_call x1, Pallas kernels: 40.7 us -> 41.8 us  [local(): pl.pallas_call(kernel, out_shape=(jax.ShapeDtypeStruct(base.shape, bf), j...]
where the time goes in v6:
time: 46.5 us; the launch traced here: 45.8 us
  Pallas kernels  45 us (97%)
  between operations  0.8 us (2%)
    pallas_call x1, Pallas kernels, local(): pl.pallas_call(kernel, out_shape=(jax.ShapeDtypeStruct(base.shape, bf), j...  41.8 us
    pallas_call x1, Pallas kernels, local(): pl.pallas_call(place, out_shape=(jax.ShapeDtypeStruct(base.shape, bf), ja...  3.23 us

profile of v6, /device:TPU:1, one launch (start us, length us, event | category | flops | bytes accessed | tf_op | source)
XLA Modules:
  0.0 45.8 jit_solution(12841532686116158462)
XLA Ops:
  0.6 41.8 %attend_all.1 = (bf16[1,128,1024]{2,1,0:T(8,128)(2,1)}, bf16[4,2,128,128]{3,2,1,0:T(8,128)(2,1)}) custom-call(s32[4,32]{1,0:T(4,128)} %table_in.1, s32[4]{0:T(128)} %plens_in.1, s32[4]{0:T(128)} %slens_in.1, s32[4]{0:T(128)} %adapters_in.1, s32[4,16]{1,0:T(4,128)} %wslots.1, bf16[1,128,1024]{2,1,0:T(8,128)(2,1)} %hidden.1, bf16[1,128,1024]{2,1,0:T(8,128)(2,1)} %base.1, ...), custom_call_target="tpu_custom_call" | custom-call | tf_op jit(solution)/shard_map/attend_all/pallas_call | solution.py:438
  42.4 3.2 %place.1 = (bf16[1,128,1024]{2,1,0:T(8,128)(2,1)}, bf16[20,2,128,128]{3,2,1,0:T(8,128)(2,1)}) custom-call(s32[4,16]{1,0:T(4,128)} %wslots.1, bf16[1,128,1024]{2,1,0:T(8,128)(2,1)} %get-tuple-element.4.attended_in, bf16[4,2,128,128]{3,2,1,0:T(8,128)(2,1)} %get-tuple-element.5.writes, bf16[20,2,128,128]{3,2,1,0:T(8,128)(2,1)} %pool.3), custom_call_target="tpu_custom_call" | custom-call | tf_op jit(solution)/shard_map/place/pallas_call | solution.py:484
